TPU v7x, 32 devices: a whole 2x2x4 slice. The times are simulated.
32 devices in a mesh: pipe: 2 (over core), ctx: 16 (over z, y, x).
Axes of the slice: x: 2, y: 2, z: 4, core: 2. Of those that a mesh axis runs over, the one named last changes fastest.
Arguments:
- t_query: bfloat16 [2, 2048, 4096], P('pipe', 'ctx'), may hold values from -33 to 33
- t_key: bfloat16 [2, 2048, 512], P('pipe', 'ctx'), may hold values from -6 to 6
- t_value: bfloat16 [2, 2048, 512], P('pipe', 'ctx'), may hold values from -6 to 6
- s_query: bfloat16 [2, 2048, 4096], P('pipe', 'ctx'), may hold values from -33 to 33
- s_key: bfloat16 [2, 2048, 512], P('pipe', 'ctx'), may hold values from -6 to 6
- s_value: bfloat16 [2, 2048, 512], P('pipe', 'ctx'), may hold values from -6 to 6
- segment_ids: int32 [2048], replicated, may hold values from 0 to 15, never falling along the last dimension, each value on 1 to 256 neighbouring positions
Outputs:
- loss: float32 [], replicated
- query_grad: float32 [2, 2048, 4096], P('pipe', 'ctx')
- key_grad: float32 [2, 2048, 512], P('pipe', 'ctx')
- value_grad: float32 [2, 2048, 512], P('pipe', 'ctx')
Inputs may be any that keep to these rules, and one draw needn't show every extreme that they name: `segment_ids`: segment ids never fall along the tokens; a document holds at most 256 tokens, and one holds exactly that many.
All inputs are finite; a program needn't handle non-finite values.
Results may differ from a plain program's by a relative error of at most 0.006.
Values may be sent and summed in bfloat16 or wider, within the bound.
A program may use at most 128 MiB of HBM per device.

v0:
```python
import jax
import jax.numpy as jnp
from jax import lax
from jax.sharding import PartitionSpec as P

REACH = 2
HEADS = 32
KV_HEADS = 4
HEAD_DIM = 128


NEG_FILL = -1e30


def shifted(block, axis, distance):
    devices = range(lax.axis_size(axis))
    route = [(i - distance, i) for i in devices if i - distance in devices]
    return lax.ppermute(block, axis, route)


def prefix(value, axis, join, neutral):
    count, mine = (lax.axis_size(axis), lax.axis_index(axis))
    pieces = lax.all_gather(value, axis)
    pieces = pieces[::-1]
    mine = count - 1 - mine
    total = jnp.full_like(value, 0) + jnp.asarray(neutral, value.dtype)

    def step(position, total):
        longer = join(total, pieces[position])
        return jnp.where(position < mine, longer, total)

    return lax.fori_loop(0, count - 1, step, total)


def scores_of(query_half, keys_half):
    tok_rows = query_half.shape[0]
    key_count = keys_half.shape[0]
    grouped = query_half.reshape(tok_rows, KV_HEADS, HEADS // KV_HEADS, HEAD_DIM)
    key_heads = keys_half.reshape(key_count, KV_HEADS, HEAD_DIM)
    return jnp.einsum(
        "rkgd,wkd->kgrw", grouped, key_heads, preferred_element_type=jnp.float32
    ) * HEAD_DIM ** (-0.5)


def forward(query_half, keys_half, values_half, allowed):
    tok_rows = query_half.shape[0]
    scores = jnp.where(allowed[None, None], scores_of(query_half, keys_half), NEG_FILL)
    row_peak = jnp.max(scores, axis=-1, keepdims=True)
    expo = jnp.exp(scores - row_peak)
    row_total = jnp.sum(expo, axis=-1, keepdims=True)
    value_heads = values_half.reshape(values_half.shape[0], KV_HEADS, HEAD_DIM)
    mixed = jnp.einsum(
        "kgrw,wkd->rkgd", expo.astype(jnp.bfloat16), value_heads, preferred_element_type=jnp.float32
    )
    mixed = mixed / jnp.transpose(row_total, (2, 0, 1, 3))
    return (mixed.reshape(tok_rows, HEADS * HEAD_DIM).astype(jnp.bfloat16), row_peak, row_total)


def add_single(earlier, later):
    return earlier + later


def per_device(t_query, t_key, t_value, s_query, s_key, s_value, segment_ids):
    tok_rows = t_query.shape[1]
    group = HEADS // KV_HEADS
    scale = HEAD_DIM ** (-0.5)
    key_pad = REACH * tok_rows
    key_span = key_pad + tok_rows
    device_pos = lax.axis_index("ctx")
    section_pos = lax.axis_index("pipe")
    own_blocks = (t_key[0], t_value[0], s_key[0], s_value[0])
    collected = [own_blocks]
    for step_by in range(1, REACH + 1):
        collected.append(
            shifted((own_blocks[0], own_blocks[1], own_blocks[2], own_blocks[3]), "ctx", step_by)
        )
    ordered = collected[::-1]
    windows = [
        jnp.concatenate([blocks[member] for blocks in ordered], axis=0) for member in range(4)
    ]
    seg_front = jnp.concatenate([jnp.full((key_pad,), -1, jnp.int32), segment_ids])
    key_seg = lax.dynamic_slice_in_dim(seg_front, device_pos * tok_rows, key_span)
    query_seg = lax.dynamic_slice_in_dim(segment_ids, device_pos * tok_rows, tok_rows)
    causal = jnp.arange(key_span)[None, :] <= jnp.arange(tok_rows)[:, None] + key_pad
    allowed = (key_seg[None, :] == query_seg[:, None]) & causal
    teacher_out, unused_peak, unused_total = forward(t_query[0], windows[0], windows[1], allowed)
    student_out, row_peak, row_total = forward(s_query[0], windows[2], windows[3], allowed)
    mapped = jnp.minimum(section_pos + 1, lax.axis_size("pipe") - 1)
    zeros_full = jnp.zeros((tok_rows, HEADS * HEAD_DIM), jnp.float32)
    student_piece = lax.all_gather(student_out[None], "pipe", axis=0, tiled=True)
    teacher_piece = lax.all_gather(teacher_out[None], "pipe", axis=0, tiled=True)
    section_ids = jnp.arange(student_piece.shape[0], dtype=jnp.int32)
    student_mark = (section_ids <= section_pos).astype(jnp.bfloat16)
    teacher_mark = (section_ids <= mapped).astype(jnp.bfloat16)
    student_sum = jnp.einsum(
        "n,nrc->rc", student_mark, student_piece, preferred_element_type=jnp.float32
    )
    teacher_sum = jnp.einsum(
        "n,nrc->rc", teacher_mark, teacher_piece, preferred_element_type=jnp.float32
    )
    gap = student_sum - teacher_sum
    total_squares = lax.psum(jnp.sum(gap * gap), ("pipe", "ctx"))
    loss = total_squares / float(
        lax.axis_size("pipe") * lax.axis_size("ctx") * tok_rows * HEADS * HEAD_DIM
    )
    after_gap = prefix(gap, "pipe", add_single, zeros_full)
    out_grad = after_gap + gap
    grad_half = out_grad.astype(jnp.bfloat16)
    grad_heads = grad_half.reshape(tok_rows, KV_HEADS, group, HEAD_DIM)
    query_heads = s_query[0].reshape(tok_rows, KV_HEADS, group, HEAD_DIM)
    key_heads = windows[2].reshape(key_span, KV_HEADS, HEAD_DIM)
    value_heads = windows[3].reshape(key_span, KV_HEADS, HEAD_DIM)
    scores = jnp.where(allowed[None, None], scores_of(s_query[0], windows[2]), NEG_FILL)
    prob = jnp.exp(scores - row_peak) / row_total
    prob_half = prob.astype(jnp.bfloat16)
    dprob = jnp.einsum(
        "rkgd,wkd->kgrw", grad_heads, value_heads, preferred_element_type=jnp.float32
    )
    out_heads = student_out.reshape(tok_rows, KV_HEADS, group, HEAD_DIM)
    delta = jnp.einsum("rkgd,rkgd->kgr", grad_heads, out_heads, preferred_element_type=jnp.float32)
    dscore = (prob * (dprob - delta[..., None])).astype(jnp.bfloat16)
    query_grad = (
        jnp.einsum("kgrw,wkd->rkgd", dscore, key_heads, preferred_element_type=jnp.float32).reshape(
            tok_rows, HEADS * HEAD_DIM
        )
        * scale
    )
    key_width = KV_HEADS * HEAD_DIM
    key_win = (
        jnp.einsum(
            "kgrw,rkgd->wkd", dscore, query_heads, preferred_element_type=jnp.float32
        ).reshape(key_span, key_width)
        * scale
    )
    value_win = jnp.einsum(
        "kgrw,rkgd->wkd", prob_half, grad_heads, preferred_element_type=jnp.float32
    ).reshape(key_span, key_width)
    key_grad = key_win[key_pad:]
    value_grad = value_win[key_pad:]
    for step_by in range(1, REACH + 1):
        first = (REACH - step_by) * tok_rows
        outgoing = (key_win[first : first + tok_rows], value_win[first : first + tok_rows])
        returned = shifted((outgoing[0], outgoing[1]), "ctx", -step_by)
        key_grad = key_grad + returned[0]
        value_grad = value_grad + returned[1]
    return (loss, query_grad[None], key_grad[None], value_grad[None])


def solution(mesh):
    placed = (
        P("pipe", "ctx", None),
        P("pipe", "ctx", None),
        P("pipe", "ctx", None),
        P("pipe", "ctx", None),
        P("pipe", "ctx", None),
        P("pipe", "ctx", None),
        P(),
    )
    return jax.shard_map(
        per_device,
        mesh=mesh,
        in_specs=placed,
        out_specs=(P(), P("pipe", "ctx", None), P("pipe", "ctx", None), P("pipe", "ctx", None)),
        check_vma=False,
    )
```

profile of v0, /device:TPU:6, one launch (start us, length us, event | category | flops | bytes accessed | tf_op | source)
XLA Modules:
  0.0 196.5 jit_solution(10387595346610605224)
XLA Ops:
  8.2 3.4 %collective-permute-start.3 = (bf16[128,512]{0,1:T(8,128)(2,1)S(1)}, bf16[128,512]{0,1:T(8,128)(2,1)S(1)}, u32[]{:S(2)}, u32[]{:S(2)}) collective-permute-start(bf16[128,512]{0,1:T(8,128)(2,1)S(1)} %bitcast.181), channel_id=1, source_target_pairs={{0,1},{1,2},{2,3},{3,4},{4,5},{5,6},{6,7},{7,8},{8,9},{9,10},{10,1... | collective-permute-start | bytes 393224 | tf_op jit(solution)/shard_map/ppermute | solution.py:18
  11.6 3.4 %collective-permute-start.2 = (bf16[128,512]{0,1:T(8,128)(2,1)S(1)}, bf16[128,512]{0,1:T(8,128)(2,1)S(1)}, u32[]{:S(2)}, u32[]{:S(2)}) collective-permute-start(bf16[128,512]{0,1:T(8,128)(2,1)S(1)} %bitcast.182), channel_id=1, source_target_pairs={{0,2},{1,3},{2,4},{3,5},{4,6},{5,7},{6,8},{7,9},{8,10},{9,11},{10,... | collective-permute-start | bytes 393224 | tf_op jit(solution)/shard_map/ppermute | solution.py:18
  16.1 3.4 %collective-permute-start.7 = (bf16[128,512]{0,1:T(8,128)(2,1)S(1)}, bf16[128,512]{0,1:T(8,128)(2,1)S(1)}, u32[]{:S(2)}, u32[]{:S(2)}) collective-permute-start(bf16[128,512]{0,1:T(8,128)(2,1)S(1)} %bitcast.178), channel_id=1, source_target_pairs={{0,1},{1,2},{2,3},{3,4},{4,5},{5,6},{6,7},{7,8},{8,9},{9,10},{10,1... | collective-permute-start | bytes 393224 | tf_op jit(solution)/shard_map/ppermute | solution.py:18
  19.5 3.4 %collective-permute-start.6 = (bf16[128,512]{0,1:T(8,128)(2,1)S(1)}, bf16[128,512]{0,1:T(8,128)(2,1)S(1)}, u32[]{:S(2)}, u32[]{:S(2)}) collective-permute-start(bf16[128,512]{0,1:T(8,128)(2,1)S(1)} %bitcast.179), channel_id=1, source_target_pairs={{0,2},{1,3},{2,4},{3,5},{4,6},{5,7},{6,8},{7,9},{8,10},{9,11},{10,... | collective-permute-start | bytes 393224 | tf_op jit(solution)/shard_map/ppermute | solution.py:18
  23.0 3.4 %collective-permute-start.5 = (bf16[128,512]{1,0:T(8,128)(2,1)}, bf16[128,512]{1,0:T(8,128)(2,1)S(1)}, u32[]{:S(2)}, u32[]{:S(2)}) collective-permute-start(bf16[128,512]{1,0:T(8,128)(2,1)} %bitcast.184), channel_id=1, source_target_pairs={{0,1},{1,2},{2,3},{3,4},{4,5},{5,6},{6,7},{7,8},{8,9},{9,10},{10,1... | collective-permute-start | bytes 393224 | tf_op jit(solution)/shard_map/ppermute | solution.py:18
  33.1 3.4 %collective-permute-start.4 = (bf16[128,512]{1,0:T(8,128)(2,1)}, bf16[128,512]{1,0:T(8,128)(2,1)}, u32[]{:S(2)}, u32[]{:S(2)}) collective-permute-start(bf16[128,512]{1,0:T(8,128)(2,1)} %bitcast.185), channel_id=1, source_target_pairs={{0,2},{1,3},{2,4},{3,5},{4,6},{5,7},{6,8},{7,9},{8,10},{9,11},{10,... | collective-permute-start | bytes 393224 | tf_op jit(solution)/shard_map/ppermute | solution.py:18
  38.2 3.4 %fusion.7 = (f32[4,8,128]{2,1,0:T(8,128)}, f32[4,8,128]{2,1,0:T(8,128)S(1)}, f32[4,384,128,8]{2,1,3,0:T(8,128)S(1)}) fusion(f32[4,384,128,8]{2,1,3,0:T(8,128)S(1)} %get-tuple-element.44, f32[4,8,128]{2,1,0:T(8,128)S(1)} %get-tuple-element.43, pred[128,384]{0,1:T(8,128)(4,1)S(1)} %fusion.53, bf16[128,4,8,128]{3,2,1,0:T(8,128)(2,1)S(1)} %bitcast.170, ...), kind=kOutput, calls=%fused_computation.12 | convolution fusion | flops 414834688 | bytes 14123008 | tf_op jit(solution)/shard_map/rkgd,wkd->kgrw/dot_general | solution.py:40
  41.5 2.6 %copy-done.2 = f32[4,384,128,8]{2,1,3,0:T(8,128)} copy-done((f32[4,384,128,8]{2,1,3,0:T(8,128)}, f32[4,384,128,8]{2,1,3,0:T(8,128)S(1)}, u32[]{:S(2)}) %copy-start.2) | copy-done | bytes 6291480
  46.8 4.6 %fusion.26 = bf16[128,4,8,128]{0,3,2,1:T(8,128)(2,1)S(1)} fusion(f32[4,384,128,8]{2,1,3,0:T(8,128)} %copy-done.2, f32[4,8,128]{2,1,0:T(8,128)S(1)} %get-tuple-element.32, pred[128,384]{0,1:T(8,128)(4,1)S(1)} %fusion.53, f32[128,4,8]{0,2,1:T(8,128)S(1)} %bitcast.201, bf16[128,4,128]{0,2,1:T(8,128)(2,1)S(1)} %bitcast.194, ...), kind=kOutput, calls=%fused_computation.33 | convolution fusion | flops 411172864 | bytes 7815168 | tf_op jit(solution)/shard_map/kgrw,wkd->rkgd/dot_general | solution.py:52
  52.8 3.4 %collective-permute-start.1 = (bf16[128,512]{1,0:T(8,128)(2,1)S(1)}, bf16[128,512]{1,0:T(8,128)(2,1)S(1)}, u32[]{:S(2)}, u32[]{:S(2)}) collective-permute-start(bf16[128,512]{1,0:T(8,128)(2,1)S(1)} %bitcast.186), channel_id=1, source_target_pairs={{0,1},{1,2},{2,3},{3,4},{4,5},{5,6},{6,7},{7,8},{8,9},{9,10},{10,1... | collective-permute-start | bytes 393224 | tf_op jit(solution)/shard_map/ppermute | solution.py:18
  56.2 3.4 %collective-permute-start = (bf16[128,512]{1,0:T(8,128)(2,1)S(1)}, bf16[128,512]{1,0:T(8,128)(2,1)S(1)}, u32[]{:S(2)}, u32[]{:S(2)}) collective-permute-start(bf16[128,512]{1,0:T(8,128)(2,1)S(1)} %bitcast.187), channel_id=1, source_target_pairs={{0,2},{1,3},{2,4},{3,5},{4,6},{5,7},{6,8},{7,9},{8,10},{9,11},{10,... | collective-permute-start | bytes 393224 | tf_op jit(solution)/shard_map/ppermute | solution.py:18
  59.9 3.1 %collective-permute-done = bf16[128,512]{1,0:T(8,128)(2,1)S(1)} collective-permute-done((bf16[128,512]{1,0:T(8,128)(2,1)S(1)}, bf16[128,512]{1,0:T(8,128)(2,1)S(1)}, u32[]{:S(2)}, u32[]{:S(2)}) %collective-permute-start) | collective-permute-done | bytes 131104 | tf_op jit(solution)/shard_map/ppermute | solution.py:18
  63.2 4.6 %fusion.27 = bf16[128,4,8,128]{0,3,2,1:T(8,128)(2,1)S(1)} fusion(f32[4,384,128,8]{2,1,3,0:T(8,128)} %copy-done.3, f32[4,8,128]{2,1,0:T(8,128)S(1)} %get-tuple-element.43, pred[128,384]{0,1:T(8,128)(4,1)} %copy-done.4, f32[128,4,8]{0,2,1:T(8,128)S(1)} %bitcast.202, bf16[128,4,128]{0,2,1:T(8,128)(2,1)S(1)} %bitcast.188, ...), kind=kOutput, calls=%fused_computation.35 | convolution fusion | flops 411172864 | bytes 7815168 | tf_op jit(solution)/shard_map/kgrw,wkd->rkgd/dot_general | solution.py:52
  69.5 5.3 %fusion.28 = f32[1,128,4096]{2,0,1:T(1,128)} fusion(bf16[2,128,4096]{2,1,0:T(8,128)(2,1)} %all-gather.7.cloned.1.call-done, s32[]{:T(128)S(6)} %min.3), kind=kOutput, calls=%fused_computation.37 | convolution fusion | flops 2097154 | bytes 4194308 | tf_op jit(solution)/shard_map/n,nrc->rc/dot_general | solution.py:98
  74.7 5.1 %copy.114 = f32[1,128,4096]{1,2,0:T(8,128)S(1)} copy(f32[1,128,4096]{2,0,1:T(1,128)} %fusion.28) | data formatting | bytes 4194304 | tf_op jit(solution)/shard_map/n,nrc->rc/dot_general | solution.py:98
  79.9 5.3 %fusion.30 = f32[1,128,4096]{2,0,1:T(1,128)} fusion(bf16[2,128,4096]{2,1,0:T(8,128)(2,1)} %all-gather.5.cloned.1.call-done, s32[]{:T(128)S(6)} %axis_index.27), kind=kOutput, calls=%fused_computation.39 | convolution fusion | flops 2097154 | bytes 4194308 | tf_op jit(solution)/shard_map/n,nrc->rc/dot_general | solution.py:95
  85.1 5.6 %copy.109 = f32[1,128,4096]{1,2,0:T(8,128)} copy(f32[1,128,4096]{2,0,1:T(1,128)} %fusion.30) | data formatting | bytes 4194304 | tf_op jit(solution)/shard_map/n,nrc->rc/dot_general | solution.py:95
  90.8 4.0 %multiply_reduce_fusion = (f32[]{:T(128)}, f32[128,4096]{0,1:T(8,128)}) fusion(f32[1,128,4096]{1,2,0:T(8,128)S(1)} %copy.114, f32[1,128,4096]{1,2,0:T(8,128)} %copy.109), kind=kLoop, calls=%fused_computation.36 | loop fusion | flops 1572863 | bytes 6291460 | tf_op jit(solution)/shard_map/reduce_sum | solution.py:102
  94.8 41.5 %psum.7 = f32[]{:T(128)} all-reduce(f32[]{:T(128)} %get-tuple-element.35), channel_id=1, replica_groups=mesh['pipe'=2,'ctx'=16] {'pipe','ctx'}, use_global_device_ids=true, to_apply=%region_5.6 | all-reduce | flops 1 | bytes 8 | tf_op jit(solution)/shard_map/psum | solution.py:102
  137.0 3.0 %fusion.25 = (f32[4,8,128]{2,1,0:T(8,128)S(1)}, bf16[128,4096]{0,1:T(8,128)(2,1)S(1)}) fusion(bf16[128,4,8,128]{0,3,2,1:T(8,128)(2,1)S(1)} %fusion.27, f32[128,4096]{0,1:T(8,128)} %get-tuple-element.36, f32[256,4096]{0,1:T(8,128)} %all-gather.9.cloned.1.call-done, pred[]{:T(512)S(6)} %lt.12), kind=kLoop, calls=%fused_computation.30 | loop fusion | flops 3665920 | bytes 6307841 | tf_op jit(solution)/shard_map/rkgd,rkgd->kgr/dot_general | solution.py:120
  140.1 5.6 %fusion.36 = f32[384,4,128]{0,2,1:T(8,128)} fusion(bf16[128,4,8,128]{0,3,2,1:T(8,128)(2,1)S(1)} %bitcast.167, f32[4,384,128,8]{2,1,3,0:T(8,128)} %copy-done.3, f32[4,8,128]{2,1,0:T(8,128)S(1)} %copy-done.16, f32[4,8,128]{2,1,0:T(8,128)S(1)} %get-tuple-element.43, pred[128,384]{0,1:T(8,128)(4,1)S(1)} %copy-done.5), kind=kOutput, calls=%fused_computation.42 | convolution fusion | flops 410517504 | bytes 8208384 | tf_op jit(solution)/shard_map/kgrw,rkgd->wkd/dot_general | solution.py:135
  145.8 2.4 %fusion.1 = bf16[4,8,128,384]{2,3,1,0:T(8,128)(2,1)S(1)} fusion(f32[4,8,128]{2,1,0:T(8,128)S(1)} %get-tuple-element.33, bf16[128,4,8,128]{0,3,2,1:T(8,128)(2,1)S(1)} %bitcast.168, f32[4,8,128]{2,1,0:T(8,128)S(1)} %copy-done.17, f32[4,8,128]{2,1,0:T(8,128)S(1)} %get-tuple-element.43, f32[4,384,128,8]{2,1,3,0:T(8,128)S(1)} %bitcast.165, ...), kind=kOutput, calls=%fused_computation.2 | convolution fusion | flops 414842880 | bytes 10977280 | tf_op jit(solution)/shard_map/rkgd,wkd->kgrw/dot_general | solution.py:116
  153.8 2.0 %fusion.71 = (f32[128,4,128]{0,2,1:T(8,128)}, f32[128,4,128]{0,2,1:T(8,128)}, f32[128,4,128]{0,2,1:T(8,128)}) fusion(f32[384,4,128]{0,2,1:T(8,128)} %fusion.36), kind=kLoop, calls=%fused_computation.85 | loop fusion | bytes 1572864 | tf_op jit(solution)/shard_map/slice | solution.py:142
  159.3 2.2 %collective-permute-start.11 = (f32[128,512]{1,0:T(8,128)}, f32[128,512]{1,0:T(8,128)}, u32[]{:S(2)}, u32[]{:S(2)}) collective-permute-start(f32[128,512]{1,0:T(8,128)} %copy.103), channel_id=1, source_target_pairs={{2,0},{3,1},{4,2},{5,3},{6,4},{7,5},{8,6},{9,7},{10,8},{11,9},{12,... | collective-permute-start | bytes 786440 | tf_op jit(solution)/shard_map/ppermute | solution.py:18
  161.6 2.1 %collective-permute-start.10 = (f32[128,512]{1,0:T(8,128)}, f32[128,512]{1,0:T(8,128)}, u32[]{:S(2)}, u32[]{:S(2)}) collective-permute-start(f32[128,512]{1,0:T(8,128)} %copy.101), channel_id=1, source_target_pairs={{1,0},{2,1},{3,2},{4,3},{5,4},{6,5},{7,6},{8,7},{9,8},{10,9},{11,1... | collective-permute-start | bytes 786440 | tf_op jit(solution)/shard_map/ppermute | solution.py:18
  163.7 1.9 collective-permute-start.9
  165.6 2.6 %collective-permute-start.8 = (f32[128,512]{1,0:T(8,128)}, f32[128,512]{1,0:T(8,128)}, u32[]{:S(2)}, u32[]{:S(2)}) collective-permute-start(f32[128,512]{1,0:T(8,128)} %copy.97), channel_id=1, source_target_pairs={{1,0},{2,1},{3,2},{4,3},{5,4},{6,5},{7,6},{8,7},{9,8},{10,9},{11,1... | collective-permute-start | bytes 786440 | tf_op jit(solution)/shard_map/ppermute | solution.py:18
  168.2 2.1 %convolution_multiply_fusion = f32[4,128,8,128]{3,1,2,0:T(8,128)} fusion(bf16[4,8,128,384]{2,3,1,0:T(8,128)(2,1)S(1)} %fusion.1, bf16[128,4,128]{2,0,1:T(8,128)(2,1)S(1)} %copy.76, bf16[128,4,128]{2,0,1:T(8,128)(2,1)S(1)} %copy.75, bf16[128,4,128]{2,0,1:T(8,128)(2,1)S(1)} %copy.74), kind=kOutput, calls=%fused_computation.41 | convolution fusion | flops 404357120 | bytes 5636096 | tf_op jit(solution)/shard_map/kgrw,wkd->rkgd/dot_general | solution.py:123
  170.3 2.9 %copy.104 = f32[1,128,4096]{2,1,0:T(8,128)} copy(f32[1,128,4096]{1,2,0:T(8,128)} %bitcast.163) | data formatting | bytes 4194304
  175.3 4.5 %collective-permute-done.11 = f32[128,512]{1,0:T(8,128)} collective-permute-done((f32[128,512]{1,0:T(8,128)}, f32[128,512]{1,0:T(8,128)}, u32[]{:S(2)}, u32[]{:S(2)}) %collective-permute-start.11) | collective-permute-done | bytes 262176 | tf_op jit(solution)/shard_map/ppermute | solution.py:18
  181.6 2.1 %collective-permute-done.9 = f32[128,512]{1,0:T(8,128)} collective-permute-done((f32[128,512]{1,0:T(8,128)}, f32[128,512]{1,0:T(8,128)}, u32[]{:S(2)}, u32[]{:S(2)}) %collective-permute-start.9) | collective-permute-done | bytes 262176 | tf_op jit(solution)/shard_map/ppermute | solution.py:18
  183.7 3.4 %collective-permute-done.8 = f32[128,512]{1,0:T(8,128)} collective-permute-done((f32[128,512]{1,0:T(8,128)}, f32[128,512]{1,0:T(8,128)}, u32[]{:S(2)}, u32[]{:S(2)}) %collective-permute-start.8) | collective-permute-done | bytes 262176 | tf_op jit(solution)/shard_map/ppermute | solution.py:18
  (91 shorter events, 31.2 us)
Async XLA Ops:
  7.2 62.3 %all-gather.7.cloned.1.call-start = ((), (), s32[]{:S(2)}) async-start(), calls=%async_computation.1 | async-start | bytes 3145728 | tf_op jit(solution)/shard_map/all_gather | solution.py:91
  8.2 24.9 %collective-permute-start.3 = (bf16[128,512]{0,1:T(8,128)(2,1)S(1)}, bf16[128,512]{0,1:T(8,128)(2,1)S(1)}, u32[]{:S(2)}, u32[]{:S(2)}) collective-permute-start(bf16[128,512]{0,1:T(8,128)(2,1)S(1)} %bitcast.181), channel_id=1, source_target_pairs={{0,1},{1,2},{2,3},{3,4},{4,5},{5,6},{6,7},{7,8},{8,9},{9,10},{10,1... | collective-permute-start | bytes 393224 | tf_op jit(solution)/shard_map/ppermute | solution.py:18
  11.6 25.1 %collective-permute-start.2 = (bf16[128,512]{0,1:T(8,128)(2,1)S(1)}, bf16[128,512]{0,1:T(8,128)(2,1)S(1)}, u32[]{:S(2)}, u32[]{:S(2)}) collective-permute-start(bf16[128,512]{0,1:T(8,128)(2,1)S(1)} %bitcast.182), channel_id=1, source_target_pairs={{0,2},{1,3},{2,4},{3,5},{4,6},{5,7},{6,8},{7,9},{8,10},{9,11},{10,... | collective-permute-start | bytes 393224 | tf_op jit(solution)/shard_map/ppermute | solution.py:18
  16.1 20.7 %collective-permute-start.7 = (bf16[128,512]{0,1:T(8,128)(2,1)S(1)}, bf16[128,512]{0,1:T(8,128)(2,1)S(1)}, u32[]{:S(2)}, u32[]{:S(2)}) collective-permute-start(bf16[128,512]{0,1:T(8,128)(2,1)S(1)} %bitcast.178), channel_id=1, source_target_pairs={{0,1},{1,2},{2,3},{3,4},{4,5},{5,6},{6,7},{7,8},{8,9},{9,10},{10,1... | collective-permute-start | bytes 393224 | tf_op jit(solution)/shard_map/ppermute | solution.py:18
  19.5 17.5 %collective-permute-start.6 = (bf16[128,512]{0,1:T(8,128)(2,1)S(1)}, bf16[128,512]{0,1:T(8,128)(2,1)S(1)}, u32[]{:S(2)}, u32[]{:S(2)}) collective-permute-start(bf16[128,512]{0,1:T(8,128)(2,1)S(1)} %bitcast.179), channel_id=1, source_target_pairs={{0,2},{1,3},{2,4},{3,5},{4,6},{5,7},{6,8},{7,9},{8,10},{9,11},{10,... | collective-permute-start | bytes 393224 | tf_op jit(solution)/shard_map/ppermute | solution.py:18
  23.0 22.6 %collective-permute-start.5 = (bf16[128,512]{1,0:T(8,128)(2,1)}, bf16[128,512]{1,0:T(8,128)(2,1)S(1)}, u32[]{:S(2)}, u32[]{:S(2)}) collective-permute-start(bf16[128,512]{1,0:T(8,128)(2,1)} %bitcast.184), channel_id=1, source_target_pairs={{0,1},{1,2},{2,3},{3,4},{4,5},{5,6},{6,7},{7,8},{8,9},{9,10},{10,1... | collective-permute-start | bytes 393224 | tf_op jit(solution)/shard_map/ppermute | solution.py:18
  33.0 8.6 %copy-start = (bf16[1,128,4096]{1,2,0:T(8,128)(2,1)}, bf16[1,128,4096]{1,2,0:T(8,128)(2,1)S(1)}, u32[]{:S(2)}) copy-start(bf16[1,128,4096]{1,2,0:T(8,128)(2,1)S(1)} %copy.134) | copy-start | bytes 3145732
  33.1 13.6 %copy-start.4 = (pred[128,384]{0,1:T(8,128)(4,1)}, pred[128,384]{0,1:T(8,128)(4,1)S(1)}, u32[]{:S(2)}) copy-start(pred[128,384]{0,1:T(8,128)(4,1)S(1)} %fusion.53) | copy-start | bytes 147460
  33.1 12.6 %collective-permute-start.4 = (bf16[128,512]{1,0:T(8,128)(2,1)}, bf16[128,512]{1,0:T(8,128)(2,1)}, u32[]{:S(2)}, u32[]{:S(2)}) collective-permute-start(bf16[128,512]{1,0:T(8,128)(2,1)} %bitcast.185), channel_id=1, source_target_pairs={{0,2},{1,3},{2,4},{3,5},{4,6},{5,7},{6,8},{7,9},{8,10},{9,11},{10,... | collective-permute-start | bytes 393224 | tf_op jit(solution)/shard_map/ppermute | solution.py:18
  38.2 3.4 %copy-start.3 = (f32[4,384,128,8]{2,1,3,0:T(8,128)}, f32[4,384,128,8]{2,1,3,0:T(8,128)S(1)}, u32[]{:S(2)}) copy-start(f32[4,384,128,8]{2,1,3,0:T(8,128)S(1)} %get-tuple-element.44) | copy-start | bytes 18874372
  46.7 6.0 %copy-start.7 = (bf16[1,128,512]{2,1,0:T(8,128)(2,1)S(1)}, bf16[1,128,512]{2,1,0:T(8,128)(2,1)}, u32[]{:S(2)}) copy-start(bf16[1,128,512]{2,1,0:T(8,128)(2,1)} %param.12) | copy-start | bytes 393220
  46.8 16.4 %copy-start.15 = (f32[4,8,128]{2,1,0:T(8,128)S(1)}, f32[4,8,128]{2,1,0:T(8,128)}, u32[]{:S(2)}) copy-start(f32[4,8,128]{2,1,0:T(8,128)} %get-tuple-element.31) | copy-start | bytes 49156
  52.7 27.2 %all-gather.5.cloned.1.call-start = ((), (), s32[]{:S(2)}) async-start(), calls=%async_computation | async-start | bytes 3145728 | tf_op jit(solution)/shard_map/all_gather | solution.py:90
  52.8 7.0 %collective-permute-start.1 = (bf16[128,512]{1,0:T(8,128)(2,1)S(1)}, bf16[128,512]{1,0:T(8,128)(2,1)S(1)}, u32[]{:S(2)}, u32[]{:S(2)}) collective-permute-start(bf16[128,512]{1,0:T(8,128)(2,1)S(1)} %bitcast.186), channel_id=1, source_target_pairs={{0,1},{1,2},{2,3},{3,4},{4,5},{5,6},{6,7},{7,8},{8,9},{9,10},{10,1... | collective-permute-start | bytes 393224 | tf_op jit(solution)/shard_map/ppermute | solution.py:18
  56.2 6.9 %collective-permute-start = (bf16[128,512]{1,0:T(8,128)(2,1)S(1)}, bf16[128,512]{1,0:T(8,128)(2,1)S(1)}, u32[]{:S(2)}, u32[]{:S(2)}) collective-permute-start(bf16[128,512]{1,0:T(8,128)(2,1)S(1)} %bitcast.187), channel_id=1, source_target_pairs={{0,2},{1,3},{2,4},{3,5},{4,6},{5,7},{6,8},{7,9},{8,10},{9,11},{10,... | collective-permute-start | bytes 393224 | tf_op jit(solution)/shard_map/ppermute | solution.py:18
  59.7 8.0 %copy-start.8 = (bf16[1,128,512]{1,2,0:T(8,128)(2,1)}, bf16[1,128,512]{1,2,0:T(8,128)(2,1)S(1)}, u32[]{:S(2)}) copy-start(bf16[1,128,512]{1,2,0:T(8,128)(2,1)S(1)} %copy.71) | copy-start | bytes 393220
  59.9 7.9 %copy-start.10 = (bf16[128,512]{0,1:T(8,128)(2,1)}, bf16[128,512]{0,1:T(8,128)(2,1)S(1)}, u32[]{:S(2)}) copy-start(bf16[128,512]{0,1:T(8,128)(2,1)S(1)} %copy.70) | copy-start | bytes 393220
  63.1 4.7 %copy-start.12 = (bf16[128,512]{0,1:T(8,128)(2,1)}, bf16[128,512]{0,1:T(8,128)(2,1)S(1)}, u32[]{:S(2)}) copy-start(bf16[128,512]{0,1:T(8,128)(2,1)S(1)} %copy.69) | copy-start | bytes 393220
  69.2 67.8 %all-gather.9.cloned.1.call-start = ((), (), s32[]{:S(2)}) async-start(), calls=%async_computation.2 | async-start | bytes 6291456 | tf_op jit(solution)/shard_map/all_gather | solution.py:23
  94.8 45.2 %copy-start.5 = (pred[128,384]{0,1:T(8,128)(4,1)S(1)}, pred[128,384]{0,1:T(8,128)(4,1)}, u32[]{:S(2)}) copy-start(pred[128,384]{0,1:T(8,128)(4,1)} %copy-done.4) | copy-start | bytes 147460
  94.8 45.2 %copy-start.16 = (f32[4,8,128]{2,1,0:T(8,128)S(1)}, f32[4,8,128]{2,1,0:T(8,128)}, u32[]{:S(2)}) copy-start(f32[4,8,128]{2,1,0:T(8,128)} %get-tuple-element.31) | copy-start | bytes 49156
  137.0 8.7 %slice-start = ((s8[6291456]{0:T(1024)(128)(4,1)}), s8[4194304]{0:T(1024)(128)(4,1)S(1)}, s32[]{:S(2)}) async-start(s8[6291456]{0:T(1024)(128)(4,1)} %bitcast.164), calls=%async_computation.3 | async-start | bytes 8388608
  140.0 5.7 %slice-start.1 = ((s8[6291456]{0:T(1024)(128)(4,1)}), s8[2097152]{0:T(1024)(128)(4,1)S(1)}, s32[]{:S(2)}) async-start(s8[6291456]{0:T(1024)(128)(4,1)} %bitcast.164), calls=%async_computation.4 | async-start | bytes 4194304
  140.0 5.7 %copy-start.6 = (pred[128,384]{0,1:T(8,128)(4,1)S(1)}, pred[128,384]{0,1:T(8,128)(4,1)}, u32[]{:S(2)}) copy-start(pred[128,384]{0,1:T(8,128)(4,1)} %copy-done.4) | copy-start | bytes 147460
  140.0 5.7 %copy-start.9 = (bf16[1,128,512]{1,2,0:T(8,128)(2,1)S(1)}, bf16[1,128,512]{1,2,0:T(8,128)(2,1)}, u32[]{:S(2)}) copy-start(bf16[1,128,512]{1,2,0:T(8,128)(2,1)} %copy-done.8) | copy-start | bytes 393220
  140.0 5.7 %copy-start.11 = (bf16[128,512]{0,1:T(8,128)(2,1)S(1)}, bf16[128,512]{0,1:T(8,128)(2,1)}, u32[]{:S(2)}) copy-start(bf16[128,512]{0,1:T(8,128)(2,1)} %copy-done.10) | copy-start | bytes 393220
  140.1 5.7 %copy-start.13 = (bf16[128,512]{0,1:T(8,128)(2,1)S(1)}, bf16[128,512]{0,1:T(8,128)(2,1)}, u32[]{:S(2)}) copy-start(bf16[128,512]{0,1:T(8,128)(2,1)} %copy-done.12) | copy-start | bytes 393220
  140.1 5.7 %copy-start.17 = (f32[4,8,128]{2,1,0:T(8,128)S(1)}, f32[4,8,128]{2,1,0:T(8,128)}, u32[]{:S(2)}) copy-start(f32[4,8,128]{2,1,0:T(8,128)} %get-tuple-element.31) | copy-start | bytes 49156
  159.3 20.5 %collective-permute-start.11 = (f32[128,512]{1,0:T(8,128)}, f32[128,512]{1,0:T(8,128)}, u32[]{:S(2)}, u32[]{:S(2)}) collective-permute-start(f32[128,512]{1,0:T(8,128)} %copy.103), channel_id=1, source_target_pairs={{2,0},{3,1},{4,2},{5,3},{6,4},{7,5},{8,6},{9,7},{10,8},{11,9},{12,... | collective-permute-start | bytes 786440 | tf_op jit(solution)/shard_map/ppermute | solution.py:18
  161.6 18.3 %collective-permute-start.10 = (f32[128,512]{1,0:T(8,128)}, f32[128,512]{1,0:T(8,128)}, u32[]{:S(2)}, u32[]{:S(2)}) collective-permute-start(f32[128,512]{1,0:T(8,128)} %copy.101), channel_id=1, source_target_pairs={{1,0},{2,1},{3,2},{4,3},{5,4},{6,5},{7,6},{8,7},{9,8},{10,9},{11,1... | collective-permute-start | bytes 786440 | tf_op jit(solution)/shard_map/ppermute | solution.py:18
  163.7 20.0 %collective-permute-start.9 = (f32[128,512]{1,0:T(8,128)}, f32[128,512]{1,0:T(8,128)}, u32[]{:S(2)}, u32[]{:S(2)}) collective-permute-start(f32[128,512]{1,0:T(8,128)} %copy.99), channel_id=1, source_target_pairs={{2,0},{3,1},{4,2},{5,3},{6,4},{7,5},{8,6},{9,7},{10,8},{11,9},{12,... | collective-permute-start | bytes 786440 | tf_op jit(solution)/shard_map/ppermute | solution.py:18
  165.6 21.5 %collective-permute-start.8 = (f32[128,512]{1,0:T(8,128)}, f32[128,512]{1,0:T(8,128)}, u32[]{:S(2)}, u32[]{:S(2)}) collective-permute-start(f32[128,512]{1,0:T(8,128)} %copy.97), channel_id=1, source_target_pairs={{1,0},{2,1},{3,2},{4,3},{5,4},{6,5},{7,6},{8,7},{9,8},{10,9},{11,1... | collective-permute-start | bytes 786440 | tf_op jit(solution)/shard_map/ppermute | solution.py:18
  (3 other events, 6.5 us)
Sparse Core Ops, SparseCore 0:
  52.8 9.0 all-gather.6
  69.3 9.9 all-gather.4
  94.9 13.6 all-gather.8
where the time goes:
time: 198 us; the launch traced here: 197 us
  local copies, waits for them, and re-layouts  41.8 us (21%)
  blocking collectives  41.5 us (21%)
  starting transfers between devices  36.4 us (18%)
  matrix products  35.3 us (18%)
  between operations  16.2 us (8%)
  waiting for transfers between devices  13.2 us (7%)
  other arithmetic  12.1 us (6%)
    psum x1, blocking collectives, per_device(): total_squares = lax.psum(jnp.sum(gap * gap), ('pipe', 'ctx'))  41.5 us
    ppermute x12, starting transfers between devices, shifted(): return lax.ppermute(block, axis, route)  36.1 us
    ppermute x12, waiting for transfers between devices, shifted(): return lax.ppermute(block, axis, route)  13.1 us
    unnamed x46, local copies, waits for them, and re-layouts  10.2 us
    dot_general x2, matrix products, forward(): jnp.einsum('kgrw,wkd->rkgd', expo.astype(jnp.bfloat16), value_heads, pref...  9.19 us
    dot_general x1, local copies, waits for them, and re-layouts, per_device(): jnp.einsum('n,nrc->rc', student_mark, student_piece, preferred_element_ty...  5.64 us
    dot_general x1, matrix products, per_device(): jnp.einsum('kgrw,rkgd->wkd', prob_half, grad_heads, preferred_element_typ...  5.61 us
    slice x3, local copies, waits for them, and re-layouts, per_device(): value_win[first:first + tok_rows]  5.57 us
  transfers between devices with their start and end apart: 15, of which 4 were waited for; matrix products, arithmetic and copies ran while one was open for 20% of the time, Pallas kernels for 0%

commit v1 on v0

v1 whole, which is shorter than its diff:
```python
import functools
import math

import jax
import jax.numpy as jnp
from jax import lax
from jax.experimental import pallas as pl
from jax.experimental.pallas import tpu as pltpu
from jax.sharding import PartitionSpec as P

HEADS = 32
KV_HEADS = 4
HEAD_DIM = 128
GROUP = HEADS // KV_HEADS
WIDE = GROUP * HEAD_DIM
PAIR = 2 * HEAD_DIM
PAIRS = GROUP // 2
TEACHER, STUDENT = 0, 1
NEG_FILL = -1e30
MESH = pl.DeviceIdType.MESH
F32 = jnp.float32
BF16 = jnp.bfloat16


def dot(a, b):
    return jnp.dot(a, b, preferred_element_type=F32)


def dot_nt(a, b):
    return lax.dot_general(a, b, (((1,), (1,)), ((), ())), preferred_element_type=F32)


def loss_rounds(count):
    bits = count.bit_length() - 1
    return [list(range(low, min(low + 2, bits))) for low in range(0, bits, 2)]


def kernel(
    count, rows, denominator,
    tq, tk, tv, sq, sk, sv, seg,
    loss_out, qg_out, kg_out, vg_out,
    win, qbuf, bias, weights, outs, rinv, dnorm, delta, ex_tx, ex_rx, qgrad,
    own_grad, far_grad, txx, rxx, tx2, rx2, loss_acc, loss_buf,
    own_sem, q_sem, qg_sem, far_send, far_recv, near_send, near_recv,
    ex_send, ex_recv, gx_send, gx_recv, g2_send, g2_recv, loss_send, loss_recv,
):
    pipe = lax.axis_index("pipe")
    me = lax.axis_index("ctx")
    odd = lax.rem(me, 2)
    partner = me + 1 - 2 * odd
    has_prev = me >= 2
    has_next = me < count - 2
    span = 3 * rows
    scale = HEAD_DIM ** (-0.5)
    to_exp2 = scale * math.log2(math.e)
    rounds = loss_rounds(count)

    def xor(value, mask):
        result = value
        for bit in range(count.bit_length() - 1):
            if mask >> bit & 1:
                here = lax.rem(value // (1 << bit), 2)
                result = result + (1 << bit) * (1 - 2 * here)
        return result

    partners = []
    for number, bits in enumerate(rounds):
        masks = [sum(1 << b for k, b in enumerate(bits) if pick >> k & 1) for pick in range(1 << len(bits))]
        flips = (0, 1) if number == 0 else (0,)
        partners.append([(f, m) for f in flips for m in masks if f or m])

    def member(number):
        bits = rounds[number]
        place = lax.rem(me // (1 << bits[0]), 1 << len(bits))
        if number == 0:
            place = place + pipe * (1 << len(bits))
        return place

    def other(flip, mask):
        return (1 - pipe if flip else pipe, xor(me, mask))

    def own_copy(chunk, which):
        g, model = divmod(chunk, 2)
        source = ((tk, tv), (sk, sv))[model][which]
        return pltpu.make_async_copy(
            source.at[0, :, pl.ds(g * HEAD_DIM, HEAD_DIM)],
            win.at[chunk, which, pl.ds(2 * rows, rows), :],
            own_sem.at[chunk, which],
        )

    def q_copy(g, model):
        return pltpu.make_async_copy(
            (tq, sq)[model].at[0, :, pl.ds(g * WIDE, WIDE)], qbuf.at[model, g], q_sem.at[model, g]
        )

    for chunk in range(2 * KV_HEADS):
        for which in range(2):
            own_copy(chunk, which).start()
    for g in range(KV_HEADS):
        for model in (STUDENT, TEACHER):
            q_copy(g, model).start()

    barrier = pltpu.get_barrier_semaphore()
    greeted = 0
    for number in range(len(rounds)):
        for flip, mask in partners[number]:
            pl.semaphore_signal(barrier, inc=1, device_id=other(flip, mask), device_id_type=MESH)
            greeted += 1

    ahead = lax.rem(me // 2, 2)
    remaining = lax.rem(me - 2 + 4 * ahead + count, count)
    pl.semaphore_signal(barrier, inc=1, device_id=(pipe, remaining), device_id_type=MESH)
    greeted += 1

    query_seg = seg[pl.ds(me, 1), :]
    query_pos = lax.broadcasted_iota(jnp.int32, (rows, rows), 1)
    key_pos = lax.broadcasted_iota(jnp.int32, (rows, rows), 0)
    for slot in range(3):
        behind = 2 - slot
        source = jnp.maximum(me - behind, 0)
        key_seg = jnp.broadcast_to(seg[pl.ds(source, 1), :].astype(F32), (rows, rows)).T
        same = key_seg == query_seg.astype(F32)
        if behind == 0:
            same = same & (key_pos <= query_pos)
        fill = jnp.where(same, 0.0, NEG_FILL)
        if behind:
            fill = jnp.where(me >= behind, fill, NEG_FILL)
        bias[pl.ds(slot * rows, rows), :] = fill

    @pl.when(me < 2)
    def _():
        win[:, :, pl.ds(0, rows), :] = jnp.zeros((2 * KV_HEADS, 2, rows, HEAD_DIM), BF16)

    loss_acc[...] = jnp.zeros_like(loss_acc)
    pl.semaphore_wait(barrier, greeted)

    def far_copy(chunk):
        return pltpu.make_async_remote_copy(
            src_ref=win.at[chunk, :, pl.ds(2 * rows, rows), :],
            dst_ref=win.at[chunk, :, pl.ds(0, rows), :],
            send_sem=far_send.at[chunk],
            recv_sem=far_recv.at[chunk],
            device_id=(pipe, me + 2),
            device_id_type=MESH,
        )

    def near_copy(chunk, slot):
        return pltpu.make_async_remote_copy(
            src_ref=win.at[chunk, :, pl.ds(slot * rows, rows), :],
            dst_ref=win.at[chunk, :, pl.ds(rows, rows), :],
            send_sem=near_send.at[chunk],
            recv_sem=near_recv.at[chunk],
            device_id=(pipe, partner),
            device_id_type=MESH,
        )

    for g in range(KV_HEADS):
        for model in (STUDENT, TEACHER):
            chunk = 2 * g + model
            own_copy(chunk, 0).wait()
            own_copy(chunk, 1).wait()

            @pl.when(has_next)
            def _():
                far_copy(chunk).start()

            @pl.when(odd == 0)
            def _():
                near_copy(chunk, 2).start()

    def ex_copy(g):
        return pltpu.make_async_remote_copy(
            src_ref=ex_tx.at[g], dst_ref=ex_rx.at[g], send_sem=ex_send.at[g], recv_sem=ex_recv.at[g],
            device_id=(1 - pipe, me), device_id_type=MESH,
        )

    def gx_copy(g):
        return pltpu.make_async_remote_copy(
            src_ref=txx.at[g], dst_ref=rxx.at[g], send_sem=gx_send.at[g], recv_sem=gx_recv.at[g],
            device_id=(pipe, partner), device_id_type=MESH,
        )

    def g2_copy(g):
        return pltpu.make_async_remote_copy(
            src_ref=tx2.at[g], dst_ref=rx2.at[g], send_sem=g2_send.at[g], recv_sem=g2_recv.at[g],
            device_id=(pipe, me - 2), device_id_type=MESH,
        )

    def qg_copy(g):
        return pltpu.make_async_copy(
            qgrad.at[g], qg_out.at[0, :, pl.ds(pl.multiple_of(g * WIDE, WIDE), WIDE)], qg_sem.at[g]
        )

    def loss_copy(number, index):
        flip, mask = partners[number][index]
        mine = member(number)
        return pltpu.make_async_remote_copy(
            src_ref=loss_buf.at[number, mine],
            dst_ref=loss_buf.at[number, mine],
            send_sem=loss_send.at[number, index],
            recv_sem=loss_recv.at[number, index],
            device_id=other(flip, mask),
            device_id_type=MESH,
        )

    def loss_start(number, value):
        loss_buf[number, member(number)] = value
        for index in range(len(partners[number])):
            loss_copy(number, index).start()

    def loss_finish(number):
        for index in range(len(partners[number])):
            loss_copy(number, index).wait()
        total = loss_buf[number, 0]
        for place in range(1, len(partners[number]) + 1):
            total = total + loss_buf[number, place]
        return total

    pipe_f = pipe.astype(F32)
    odd_f = odd.astype(F32)

    def query_pair(model, g, hp):
        first = qbuf[model, g, :, pl.ds(hp * PAIR, HEAD_DIM)]
        second = qbuf[model, g, :, pl.ds(hp * PAIR + HEAD_DIM, HEAD_DIM)]
        return jnp.concatenate([first, second], axis=0)

    def forward(g):
        for model in (STUDENT, TEACHER):
            chunk = 2 * g + model

            @pl.when(has_prev)
            def _():
                far_copy(chunk).wait_recv()

            @pl.when(odd == 1)
            def _():
                near_copy(chunk, 0).start()

        slot = lax.rem(g, 2)
        for model in (STUDENT, TEACHER):
            chunk = 2 * g + model
            near_copy(chunk, 0).wait_recv()
            pltpu.make_async_copy(
                (tq, sq)[model].at[0, :, pl.ds(0, WIDE)], qbuf.at[model, g], q_sem.at[model, g]
            ).wait()
            keys = win[chunk, 0]
            values_t = win[chunk, 1].T
            for hp in range(PAIRS):
                cols = pl.ds(hp * PAIR, PAIR)
                fill = bias[...]
                scores = dot_nt(keys, query_pair(model, g, hp)) + jnp.concatenate([fill, fill], axis=1)
                peak = jnp.max(scores, axis=0, keepdims=True)
                expo = jnp.exp2((scores - peak) * to_exp2)
                inverse = 1.0 / jnp.sum(expo, axis=0, keepdims=True)
                half = expo.astype(BF16)
                if model == STUDENT:
                    weights[slot, :, cols] = half
                    rinv[g, :, cols] = inverse
                mixed = (dot(values_t, half) * inverse).astype(BF16)
                outs[model, g, :, cols] = mixed
                if model == TEACHER:
                    student = outs[STUDENT, g, :, cols].astype(F32)
                    ex_tx[g, :, cols] = (student - (1.0 + pipe_f) * mixed.astype(F32)).astype(BF16)
        ex_copy(g).start()

    def backward(g):
        slot = lax.rem(g, 2)
        chunk = 2 * g + STUDENT
        ex_copy(g).wait_recv()
        squares = jnp.zeros((8, PAIR), F32)
        for hp in range(PAIRS):
            cols = pl.ds(hp * PAIR, PAIR)
            student = outs[STUDENT, g, :, cols].astype(F32)
            teacher = outs[TEACHER, g, :, cols].astype(F32)
            taken = ex_rx[g, :, cols].astype(F32)
            apart = student - teacher
            first = taken - teacher
            second = taken + apart
            both = first * first + second * second
            squares = squares + jnp.sum(both.reshape(HEAD_DIM // 8, 8, PAIR), axis=0)
            grad = ((2.0 - pipe_f) * apart + taken) * rinv[g, :, cols]
            grad = grad.astype(BF16)
            dnorm[:, cols] = grad
            delta[:, cols] = jnp.sum(grad.astype(F32) * student, axis=0, keepdims=True)
        loss_acc[...] += pipe_f * (squares[:, :HEAD_DIM] + squares[:, HEAD_DIM:])

        @pl.when(g == KV_HEADS - 1)
        def _():
            loss_start(0, loss_acc[...])

        value_win = dot_nt(weights[slot], dnorm[...])
        keys_t = win[chunk, 0].T
        values = win[chunk, 1]
        key_win = jnp.zeros((span, HEAD_DIM), F32)
        for hp in range(PAIRS):
            cols = pl.ds(hp * PAIR, PAIR)
            dprob = dot(values, dnorm[:, cols])
            dscore = (weights[slot, :, cols].astype(F32) * (dprob - delta[:, cols])).astype(BF16)
            key_win = key_win + dot(dscore, query_pair(STUDENT, g, hp))
            query_t = dot(keys_t, dscore) * scale
            qgrad[g, :, pl.ds(hp * PAIR, HEAD_DIM)] = query_t[:, :HEAD_DIM].T
            qgrad[g, :, pl.ds(hp * PAIR + HEAD_DIM, HEAD_DIM)] = query_t[:, HEAD_DIM:].T
        qg_copy(g).start()
        key_win = key_win * scale
        for which, grads in enumerate((key_win, value_win)):
            far_grad[g, which] = grads[:rows]
            txx[g, which] = grads[rows : 2 * rows].astype(BF16)
            own_grad[g, which] = grads[2 * rows :]
        gx_copy(g).start()

    def pass_on(g):
        gx_copy(g).wait_recv()
        tx2[g] = (far_grad[g] + odd_f * rxx[g].astype(F32)).astype(BF16)

        @pl.when(has_prev)
        def _():
            g2_copy(g).start()

    def step(g, carry):
        @pl.when(g < KV_HEADS)
        def _():
            forward(g)

        @pl.when(g >= 1)
        def _():
            backward(g - 1)

        @pl.when(g >= 2)
        def _():
            pass_on(g - 2)

        return carry

    lax.fori_loop(0, KV_HEADS + 1, step, 0)
    pass_on(KV_HEADS - 1)

    @pl.when(me >= count - 2)
    def _():
        rx2[...] = jnp.zeros_like(rx2)

    for number in range(1, len(rounds)):
        loss_start(number, loss_finish(number - 1))
    for g in range(KV_HEADS):
        if g == KV_HEADS - 1:
            loss_out[0, 0] = jnp.sum(loss_finish(len(rounds) - 1)) / denominator

        @pl.when(has_next)
        def _():
            g2_copy(g).wait_recv()

        cols = pl.ds(g * HEAD_DIM, HEAD_DIM)
        for which, out in enumerate((kg_out, vg_out)):
            out[0, :, cols] = (
                own_grad[g, which] + rx2[g, which].astype(F32) + (1.0 - odd_f) * rxx[g, which].astype(F32)
            )

    for chunk in range(2 * KV_HEADS):
        near_copy(chunk, 0).wait_send()

        @pl.when(has_next)
        def _():
            far_copy(chunk).wait_send()

    for g in range(KV_HEADS):
        ex_copy(g).wait_send()
        gx_copy(g).wait_send()
        qg_copy(g).wait()

        @pl.when(has_prev)
        def _():
            g2_copy(g).wait_send()


def per_device(count, pipes, t_query, t_key, t_value, s_query, s_key, s_value, segment_ids):
    rows = t_query.shape[1]
    span = 3 * rows
    width = KV_HEADS * HEAD_DIM
    denominator = float(pipes * count * rows * HEADS * HEAD_DIM)
    rounds = len(loss_rounds(count))
    dma = pltpu.SemaphoreType.DMA
    anywhere = pl.BlockSpec(memory_space=pl.ANY)
    vmem = pl.BlockSpec(memory_space=pltpu.VMEM)
    loss, query_grad, key_grad, value_grad = pl.pallas_call(
        functools.partial(kernel, count, rows, denominator),
        out_shape=(
            jax.ShapeDtypeStruct((1, 1), F32),
            jax.ShapeDtypeStruct((1, rows, HEADS * HEAD_DIM), F32),
            jax.ShapeDtypeStruct((1, rows, width), F32),
            jax.ShapeDtypeStruct((1, rows, width), F32),
        ),
        in_specs=[anywhere] * 6 + [vmem],
        out_specs=(pl.BlockSpec(memory_space=pltpu.SMEM), anywhere, vmem, vmem),
        scratch_shapes=[
            pltpu.VMEM((2 * KV_HEADS, 2, span, HEAD_DIM), BF16),
            pltpu.VMEM((2, KV_HEADS, rows, WIDE), BF16),
            pltpu.VMEM((span, rows), F32),
            pltpu.VMEM((2, span, WIDE), BF16),
            pltpu.VMEM((2, KV_HEADS, HEAD_DIM, WIDE), BF16),
            pltpu.VMEM((KV_HEADS, 1, WIDE), F32),
            pltpu.VMEM((HEAD_DIM, WIDE), BF16),
            pltpu.VMEM((1, WIDE), F32),
            pltpu.VMEM((KV_HEADS, HEAD_DIM, WIDE), BF16),
            pltpu.VMEM((KV_HEADS, HEAD_DIM, WIDE), BF16),
            pltpu.VMEM((KV_HEADS, rows, WIDE), F32),
            pltpu.VMEM((KV_HEADS, 2, rows, HEAD_DIM), F32),
            pltpu.VMEM((KV_HEADS, 2, rows, HEAD_DIM), F32),
            pltpu.VMEM((KV_HEADS, 2, rows, HEAD_DIM), BF16),
            pltpu.VMEM((KV_HEADS, 2, rows, HEAD_DIM), BF16),
            pltpu.VMEM((KV_HEADS, 2, rows, HEAD_DIM), BF16),
            pltpu.VMEM((KV_HEADS, 2, rows, HEAD_DIM), BF16),
            pltpu.VMEM((8, HEAD_DIM), F32),
            pltpu.VMEM((rounds, 8, 8, HEAD_DIM), F32),
            dma((2 * KV_HEADS, 2)),
            dma((2, KV_HEADS)),
            dma((KV_HEADS,)),
            dma((2 * KV_HEADS,)),
            dma((2 * KV_HEADS,)),
            dma((2 * KV_HEADS,)),
            dma((2 * KV_HEADS,)),
            dma((KV_HEADS,)),
            dma((KV_HEADS,)),
            dma((KV_HEADS,)),
            dma((KV_HEADS,)),
            dma((KV_HEADS,)),
            dma((KV_HEADS,)),
            dma((rounds, 8)),
            dma((rounds, 8)),
        ],
        compiler_params=pltpu.CompilerParams(
            collective_id=0, has_side_effects=True, vmem_limit_bytes=40 * 1024 * 1024
        ),
        cost_estimate=pl.CostEstimate(
            flops=8 * 2 * HEADS * rows * span * HEAD_DIM,
            bytes_accessed=6 * 1024 * 1024,
            transcendentals=2 * HEADS * rows * span,
        ),
    )(t_query, t_key, t_value, s_query, s_key, s_value, segment_ids.reshape(count, rows))
    return loss.reshape(()), query_grad, key_grad, value_grad


def solution(mesh):
    spread = P("pipe", "ctx", None)
    return jax.shard_map(
        functools.partial(per_device, mesh.shape["ctx"], mesh.shape["pipe"]),
        mesh=mesh,
        in_specs=(spread,) * 6 + (P(),),
        out_specs=(P(), spread, spread, spread),
        check_vma=False,
    )
```

time: 198 us -> 55.6 us (0.28)
  the two profiles are of different devices: /device:TPU:6 before, /device:TPU:0 now
where the time goes in v1:
time: 55.6 us; the launch traced here: 55.3 us
  Pallas kernels  43.5 us (78%)
  local copies, waits for them, and re-layouts  9.48 us (17%)
  between operations  2.34 us (4%)
    pallas_call x1, Pallas kernels, per_device(): pl.pallas_call(functools.partial(kernel, count, rows, denominator), out_s...  43.5 us
    unnamed x17, local copies, waits for them, and re-layouts  9.48 us

profile of v1, /device:TPU:0, one launch (start us, length us, event | category | flops | bytes accessed | tf_op | source)
XLA Modules:
  0.0 55.3 jit_solution(11664118804265678812)
XLA Ops:
  0.6 0.0 copy-start
  0.6 1.2 %copy-done = bf16[1,128,4096]{2,1,0:T(8,128)(2,1)S(1)} copy-done((bf16[1,128,4096]{2,1,0:T(8,128)(2,1)S(1)}, bf16[1,128,4096]{2,1,0:T(8,128)(2,1)}, u32[]{:S(2)}) %copy-start) | copy-done | bytes 1048600
  1.9 0.0 copy-start.1
  1.9 1.2 %copy-done.1 = bf16[1,128,4096]{2,1,0:T(8,128)(2,1)S(1)} copy-done((bf16[1,128,4096]{2,1,0:T(8,128)(2,1)S(1)}, bf16[1,128,4096]{2,1,0:T(8,128)(2,1)}, u32[]{:S(2)}) %copy-start.1) | copy-done | bytes 1048600
  3.1 0.0 copy-start.2
  3.1 0.9 %copy-done.2 = bf16[1,128,512]{2,1,0:T(8,128)(2,1)S(1)} copy-done((bf16[1,128,512]{2,1,0:T(8,128)(2,1)S(1)}, bf16[1,128,512]{2,1,0:T(8,128)(2,1)}, u32[]{:S(2)}) %copy-start.2) | copy-done | bytes 131096
  4.0 0.0 copy-start.3
  4.0 0.9 %copy-done.3 = bf16[1,128,512]{2,1,0:T(8,128)(2,1)S(1)} copy-done((bf16[1,128,512]{2,1,0:T(8,128)(2,1)S(1)}, bf16[1,128,512]{2,1,0:T(8,128)(2,1)}, u32[]{:S(2)}) %copy-start.3) | copy-done | bytes 131096
  4.9 0.0 copy-start.4
  4.9 0.9 %copy-done.4 = bf16[1,128,512]{2,1,0:T(8,128)(2,1)S(1)} copy-done((bf16[1,128,512]{2,1,0:T(8,128)(2,1)S(1)}, bf16[1,128,512]{2,1,0:T(8,128)(2,1)}, u32[]{:S(2)}) %copy-start.4) | copy-done | bytes 131096
  5.8 0.0 copy-start.5
  5.8 0.9 %copy-done.5 = bf16[1,128,512]{2,1,0:T(8,128)(2,1)S(1)} copy-done((bf16[1,128,512]{2,1,0:T(8,128)(2,1)S(1)}, bf16[1,128,512]{2,1,0:T(8,128)(2,1)}, u32[]{:S(2)}) %copy-start.5) | copy-done | bytes 131096
  6.7 0.0 copy-start.6
  6.7 0.7 %copy-done.6 = s32[2048]{0:T(1024)S(1)} copy-done((s32[2048]{0:T(1024)S(1)}, s32[2048]{0:T(1024)}, u32[]{:S(2)}) %copy-start.6) | copy-done | bytes 8216
  7.4 43.5 %shard_map.102 = (f32[1,1]{1,0:T(1,128)}, f32[1,128,4096]{2,1,0:T(8,128)S(1)}, f32[1,128,512]{2,1,0:T(8,128)S(1)}, f32[1,128,512]{2,1,0:T(8,128)S(1)}) custom-call(bf16[1,128,4096]{2,1,0:T(8,128)(2,1)S(1)} %copy-done, bf16[1,128,512]{2,1,0:T(8,128)(2,1)S(1)} %copy-done.2, bf16[1,128,512]{2,1,0:T(8,128)(2,1)S(1)} %copy-done.3, ...), custom_call_target="tpu_custom_call" | custom-call | flops 3221225472 | bytes 6291456 | tf_op jit(solution)/shard_map/pallas_call | solution.py:383
  51.5 1.3 %copy.16 = f32[1,128,4096]{2,1,0:T(8,128)} copy(f32[1,128,4096]{2,1,0:T(8,128)S(1)} %get-tuple-element.17) | data formatting | bytes 4194304
  52.8 0.7 %copy.17 = f32[1,128,512]{2,1,0:T(8,128)} copy(f32[1,128,512]{2,1,0:T(8,128)S(1)} %get-tuple-element.18) | data formatting | bytes 524288
  53.5 0.7 %copy.18 = f32[1,128,512]{2,1,0:T(8,128)} copy(f32[1,128,512]{2,1,0:T(8,128)S(1)} %get-tuple-element.19) | data formatting | bytes 524288
Async XLA Ops:
  0.6 1.2 %copy-start = (bf16[1,128,4096]{2,1,0:T(8,128)(2,1)S(1)}, bf16[1,128,4096]{2,1,0:T(8,128)(2,1)}, u32[]{:S(2)}) copy-start(bf16[1,128,4096]{2,1,0:T(8,128)(2,1)} %tq.1) | copy-start | bytes 3145732
  1.9 1.2 %copy-start.1 = (bf16[1,128,4096]{2,1,0:T(8,128)(2,1)S(1)}, bf16[1,128,4096]{2,1,0:T(8,128)(2,1)}, u32[]{:S(2)}) copy-start(bf16[1,128,4096]{2,1,0:T(8,128)(2,1)} %sq.1) | copy-start | bytes 3145732
  3.1 0.9 %copy-start.2 = (bf16[1,128,512]{2,1,0:T(8,128)(2,1)S(1)}, bf16[1,128,512]{2,1,0:T(8,128)(2,1)}, u32[]{:S(2)}) copy-start(bf16[1,128,512]{2,1,0:T(8,128)(2,1)} %tk.1) | copy-start | bytes 393220
  4.0 0.9 %copy-start.3 = (bf16[1,128,512]{2,1,0:T(8,128)(2,1)S(1)}, bf16[1,128,512]{2,1,0:T(8,128)(2,1)}, u32[]{:S(2)}) copy-start(bf16[1,128,512]{2,1,0:T(8,128)(2,1)} %tv.1) | copy-start | bytes 393220
  4.9 0.9 %copy-start.4 = (bf16[1,128,512]{2,1,0:T(8,128)(2,1)S(1)}, bf16[1,128,512]{2,1,0:T(8,128)(2,1)}, u32[]{:S(2)}) copy-start(bf16[1,128,512]{2,1,0:T(8,128)(2,1)} %sk.1) | copy-start | bytes 393220
  5.8 0.9 %copy-start.5 = (bf16[1,128,512]{2,1,0:T(8,128)(2,1)S(1)}, bf16[1,128,512]{2,1,0:T(8,128)(2,1)}, u32[]{:S(2)}) copy-start(bf16[1,128,512]{2,1,0:T(8,128)(2,1)} %sv.1) | copy-start | bytes 393220
  6.7 0.7 %copy-start.6 = (s32[2048]{0:T(1024)S(1)}, s32[2048]{0:T(1024)}, u32[]{:S(2)}) copy-start(s32[2048]{0:T(1024)} %param.13) | copy-start | bytes 24580

commit v2 on v1

--- a/solution.py
+++ b/solution.py
@@ -39,7 +39,7 @@
     count, rows, denominator,
     tq, tk, tv, sq, sk, sv, seg,
     loss_out, qg_out, kg_out, vg_out,
-    win, qbuf, bias, weights, outs, rinv, dnorm, delta, ex_tx, ex_rx, qgrad,
+    win, qbuf, bias, weights, outs, rinv, dnorm, delta, dscore, ex_tx, ex_rx, qgrad,
     own_grad, far_grad, txx, rxx, tx2, rx2, loss_acc, loss_buf,
     own_sem, q_sem, qg_sem, far_send, far_recv, near_send, near_recv,
     ex_send, ex_recv, gx_send, gx_recv, g2_send, g2_recv, loss_send, loss_recv,
@@ -50,7 +50,6 @@
     partner = me + 1 - 2 * odd
     has_prev = me >= 2
     has_next = me < count - 2
-    span = 3 * rows
     scale = HEAD_DIM ** (-0.5)
     to_exp2 = scale * math.log2(math.e)
     rounds = loss_rounds(count)
@@ -112,20 +111,18 @@
     pl.semaphore_signal(barrier, inc=1, device_id=(pipe, remaining), device_id_type=MESH)
     greeted += 1
 
-    query_seg = seg[pl.ds(me, 1), :]
+    query_seg = seg[pl.ds(me, 1), :].astype(F32)
     query_pos = lax.broadcasted_iota(jnp.int32, (rows, rows), 1)
     key_pos = lax.broadcasted_iota(jnp.int32, (rows, rows), 0)
-    for slot in range(3):
-        behind = 2 - slot
+
+    def fill_of(behind):
         source = jnp.maximum(me - behind, 0)
         key_seg = jnp.broadcast_to(seg[pl.ds(source, 1), :].astype(F32), (rows, rows)).T
-        same = key_seg == query_seg.astype(F32)
-        if behind == 0:
-            same = same & (key_pos <= query_pos)
-        fill = jnp.where(same, 0.0, NEG_FILL)
-        if behind:
-            fill = jnp.where(me >= behind, fill, NEG_FILL)
-        bias[pl.ds(slot * rows, rows), :] = fill
+        fill = jnp.where(key_seg == query_seg, 0.0, NEG_FILL)
+        return jnp.where(me >= behind, fill, NEG_FILL)
+
+    bias[pl.ds(0, rows), :] = fill_of(1)
+    bias[pl.ds(rows, rows), :] = jnp.where(key_pos <= query_pos, fill_of(0), fill_of(2))
 
     @pl.when(me < 2)
     def _():
@@ -224,6 +221,9 @@
         second = qbuf[model, g, :, pl.ds(hp * PAIR + HEAD_DIM, HEAD_DIM)]
         return jnp.concatenate([first, second], axis=0)
 
+    def wide_iota(axis):
+        return lax.broadcasted_iota(jnp.int32, (rows, PAIR), axis)
+
     def forward(g):
         for model in (STUDENT, TEACHER):
             chunk = 2 * g + model
@@ -236,31 +236,58 @@
             def _():
                 near_copy(chunk, 0).start()
 
-        slot = lax.rem(g, 2)
         for model in (STUDENT, TEACHER):
-            chunk = 2 * g + model
-            near_copy(chunk, 0).wait_recv()
+            near_copy(2 * g + model, 0).wait_recv()
             pltpu.make_async_copy(
                 (tq, sq)[model].at[0, :, pl.ds(0, WIDE)], qbuf.at[model, g], q_sem.at[model, g]
             ).wait()
-            keys = win[chunk, 0]
-            values_t = win[chunk, 1].T
-            for hp in range(PAIRS):
-                cols = pl.ds(hp * PAIR, PAIR)
-                fill = bias[...]
-                scores = dot_nt(keys, query_pair(model, g, hp)) + jnp.concatenate([fill, fill], axis=1)
-                peak = jnp.max(scores, axis=0, keepdims=True)
-                expo = jnp.exp2((scores - peak) * to_exp2)
-                inverse = 1.0 / jnp.sum(expo, axis=0, keepdims=True)
-                half = expo.astype(BF16)
-                if model == STUDENT:
-                    weights[slot, :, cols] = half
-                    rinv[g, :, cols] = inverse
-                mixed = (dot(values_t, half) * inverse).astype(BF16)
-                outs[model, g, :, cols] = mixed
-                if model == TEACHER:
-                    student = outs[STUDENT, g, :, cols].astype(F32)
-                    ex_tx[g, :, cols] = (student - (1.0 + pipe_f) * mixed.astype(F32)).astype(BF16)
+
+        slot = lax.rem(g, 2)
+        triangle = wide_iota(0) <= lax.rem(wide_iota(1), rows)
+        steps = [(model, hp) for model in (STUDENT, TEACHER) for hp in range(PAIRS)]
+
+        def raw_scores(model, hp):
+            return dot_nt(win[2 * g + model, 0], query_pair(model, g, hp))
+
+        def finish(model, hp, mixed, inverse):
+            cols = pl.ds(hp * PAIR, PAIR)
+            mixed = (mixed * inverse).astype(BF16)
+            outs[model, g, :, cols] = mixed
+            if model == TEACHER:
+                student = outs[STUDENT, g, :, cols].astype(F32)
+                ex_tx[g, :, cols] = (student - (1.0 + pipe_f) * mixed.astype(F32)).astype(BF16)
+
+        values_t = [win[2 * g + model, 1].T for model in (TEACHER, STUDENT)]
+        later = raw_scores(*steps[0])
+        pending = None
+        for index, (model, hp) in enumerate(steps):
+            cols = pl.ds(hp * PAIR, PAIR)
+            raw = later
+            if index + 1 < len(steps):
+                later = raw_scores(*steps[index + 1])
+            fill = bias[pl.ds(0, rows), :]
+            middle = raw[rows : 2 * rows] + jnp.concatenate([fill, fill], axis=1)
+            fill = bias[pl.ds(rows, rows), :]
+            edge = jnp.where(triangle, raw[2 * rows :], raw[:rows]) + jnp.concatenate([fill, fill], axis=1)
+            peak = jnp.max(jnp.maximum(middle, edge), axis=0, keepdims=True)
+            middle = jnp.exp2((middle - peak) * to_exp2)
+            edge = jnp.exp2((edge - peak) * to_exp2)
+            inverse = 1.0 / jnp.sum(middle + edge, axis=0, keepdims=True)
+            half = jnp.concatenate(
+                [
+                    jnp.where(triangle, 0.0, edge).astype(BF16),
+                    middle.astype(BF16),
+                    jnp.where(triangle, edge, 0.0).astype(BF16),
+                ],
+                axis=0,
+            )
+            if model == STUDENT:
+                weights[slot, :, cols] = half
+                rinv[g, :, cols] = inverse
+            if pending is not None:
+                finish(*pending)
+            pending = (model, hp, dot(values_t[model], half), inverse)
+        finish(*pending)
         ex_copy(g).start()
 
     def backward(g):
@@ -288,25 +315,33 @@
         def _():
             loss_start(0, loss_acc[...])
 
-        value_win = dot_nt(weights[slot], dnorm[...])
-        keys_t = win[chunk, 0].T
-        values = win[chunk, 1]
-        key_win = jnp.zeros((span, HEAD_DIM), F32)
+        def dprob_of(hp):
+            return dot(win[chunk, 1], dnorm[:, pl.ds(hp * PAIR, PAIR)])
+
+        later = dprob_of(0)
         for hp in range(PAIRS):
             cols = pl.ds(hp * PAIR, PAIR)
-            dprob = dot(values, dnorm[:, cols])
-            dscore = (weights[slot, :, cols].astype(F32) * (dprob - delta[:, cols])).astype(BF16)
-            key_win = key_win + dot(dscore, query_pair(STUDENT, g, hp))
-            query_t = dot(keys_t, dscore) * scale
-            qgrad[g, :, pl.ds(hp * PAIR, HEAD_DIM)] = query_t[:, :HEAD_DIM].T
-            qgrad[g, :, pl.ds(hp * PAIR + HEAD_DIM, HEAD_DIM)] = query_t[:, HEAD_DIM:].T
-        qg_copy(g).start()
-        key_win = key_win * scale
+            dprob = later
+            if hp + 1 < PAIRS:
+                later = dprob_of(hp + 1)
+            else:
+                value_win = dot_nt(weights[slot], dnorm[...])
+            dscore[:, cols] = (weights[slot, :, cols].astype(F32) * (dprob - delta[:, cols])).astype(BF16)
+        queries = jnp.concatenate(
+            [qbuf[STUDENT, g, :, pl.ds(h * HEAD_DIM, HEAD_DIM)] for h in range(GROUP)], axis=0
+        )
+        key_win = dot(dscore[...], queries) * scale
         for which, grads in enumerate((key_win, value_win)):
             far_grad[g, which] = grads[:rows]
             txx[g, which] = grads[rows : 2 * rows].astype(BF16)
             own_grad[g, which] = grads[2 * rows :]
         gx_copy(g).start()
+        keys_t = win[chunk, 0].T
+        for hp in range(PAIRS):
+            query_t = dot(keys_t, dscore[:, pl.ds(hp * PAIR, PAIR)]) * scale
+            qgrad[g, :, pl.ds(hp * PAIR, HEAD_DIM)] = query_t[:, :HEAD_DIM].T
+            qgrad[g, :, pl.ds(hp * PAIR + HEAD_DIM, HEAD_DIM)] = query_t[:, HEAD_DIM:].T
+        qg_copy(g).start()
 
     def pass_on(g):
         gx_copy(g).wait_recv()
@@ -378,7 +413,7 @@
     denominator = float(pipes * count * rows * HEADS * HEAD_DIM)
     rounds = len(loss_rounds(count))
     dma = pltpu.SemaphoreType.DMA
-    anywhere = pl.BlockSpec(memory_space=pl.ANY)
+    anywhere = pl.BlockSpec(memory_space=pltpu.HBM)
     vmem = pl.BlockSpec(memory_space=pltpu.VMEM)
     loss, query_grad, key_grad, value_grad = pl.pallas_call(
         functools.partial(kernel, count, rows, denominator),
@@ -393,12 +428,13 @@
         scratch_shapes=[
             pltpu.VMEM((2 * KV_HEADS, 2, span, HEAD_DIM), BF16),
             pltpu.VMEM((2, KV_HEADS, rows, WIDE), BF16),
-            pltpu.VMEM((span, rows), F32),
+            pltpu.VMEM((2 * rows, rows), F32),
             pltpu.VMEM((2, span, WIDE), BF16),
             pltpu.VMEM((2, KV_HEADS, HEAD_DIM, WIDE), BF16),
             pltpu.VMEM((KV_HEADS, 1, WIDE), F32),
             pltpu.VMEM((HEAD_DIM, WIDE), BF16),
             pltpu.VMEM((1, WIDE), F32),
+            pltpu.VMEM((span, WIDE), BF16),
             pltpu.VMEM((KV_HEADS, HEAD_DIM, WIDE), BF16),
             pltpu.VMEM((KV_HEADS, HEAD_DIM, WIDE), BF16),
             pltpu.VMEM((KV_HEADS, rows, WIDE), F32),
@@ -427,7 +463,7 @@
             dma((rounds, 8)),
         ],
         compiler_params=pltpu.CompilerParams(
-            collective_id=0, has_side_effects=True, vmem_limit_bytes=40 * 1024 * 1024
+            collective_id=0, has_side_effects=True, vmem_limit_bytes=60 * 1024 * 1024
         ),
         cost_estimate=pl.CostEstimate(
             flops=8 * 2 * HEADS * rows * span * HEAD_DIM,

time: 55.6 us -> 48.5 us (0.87)
  local copies, waits for them, and re-layouts: 9.48 us -> 4.58 us
  Pallas kernels: 43.5 us -> 41.3 us
    unnamed x17 -> x7, local copies, waits for them, and re-layouts: 9.48 us -> 4.58 us
    pallas_call x1, Pallas kernels: 43.5 us -> 41.3 us  [per_device(): pl.pallas_call(functools.partial(kernel, count, rows, denominator), out_s...]
where the time goes in v2:
time: 48.5 us; the launch traced here: 48.3 us
  Pallas kernels  41.3 us (85%)
  local copies, waits for them, and re-layouts  4.58 us (9%)
  between operations  2.46 us (5%)
    pallas_call x1, Pallas kernels, per_device(): pl.pallas_call(functools.partial(kernel, count, rows, denominator), out_s...  41.3 us
    unnamed x7, local copies, waits for them, and re-layouts  4.58 us

profile of v2, /device:TPU:0, one launch (start us, length us, event | category | flops | bytes accessed | tf_op | source)
XLA Modules:
  0.0 48.3 jit_solution(9730166487357337459)
XLA Ops:
  0.6 41.3 %shard_map.102 = (f32[1,1]{1,0:T(1,128)}, f32[1,128,4096]{2,1,0:T(8,128)}, f32[1,128,512]{2,1,0:T(8,128)}, f32[1,128,512]{2,1,0:T(8,128)}) custom-call(bf16[1,128,4096]{2,1,0:T(8,128)(2,1)} %tq.1, bf16[1,128,512]{2,1,0:T(8,128)(2,1)} %tk.1, bf16[1,128,512]{2,1,0:T(8,128)(2,1)} %tv.1, bf16[1,128,4096]{2,1,0:T(8,128)(2,1)} %sq.1, bf16[1,128,512]{2,1,0:T(8,128)(2,1)} %sk.1, ...), custom_call_target="tpu_custom_call" | custom-call | flops 3221225472 | bytes 6291456 | tf_op jit(solution)/shard_map/pallas_call | solution.py:418
  42.6 0.0 copy-start.1
  42.6 0.0 copy-start
  42.6 3.2 %copy.16 = f32[1,128,4096]{2,1,0:T(8,128)} copy(f32[1,128,4096]{2,1,0:T(8,128)} %get-tuple-element.17) | data formatting | bytes 4194304
  45.8 0.0 copy-done.1
  45.8 0.7 %copy.17 = f32[1,128,512]{2,1,0:T(8,128)} copy(f32[1,128,512]{2,1,0:T(8,128)S(1)} %copy-done.1) | data formatting | bytes 524288
  46.5 0.0 copy-done
  46.5 0.7 %copy.18 = f32[1,128,512]{2,1,0:T(8,128)} copy(f32[1,128,512]{2,1,0:T(8,128)S(1)} %copy-done) | data formatting | bytes 524288
Async XLA Ops:
  42.6 3.2 %copy-start.1 = (f32[1,128,512]{2,1,0:T(8,128)S(1)}, f32[1,128,512]{2,1,0:T(8,128)}, u32[]{:S(2)}) copy-start(f32[1,128,512]{2,1,0:T(8,128)} %get-tuple-element.18) | copy-start | bytes 786436
  42.6 3.9 %copy-start = (f32[1,128,512]{2,1,0:T(8,128)S(1)}, f32[1,128,512]{2,1,0:T(8,128)}, u32[]{:S(2)}) copy-start(f32[1,128,512]{2,1,0:T(8,128)} %get-tuple-element.19) | copy-start | bytes 786436

commit v3 on v2

--- a/solution.py
+++ b/solution.py
@@ -17,6 +17,7 @@
 PAIRS = GROUP // 2
 TEACHER, STUDENT = 0, 1
 NEG_FILL = -1e30
+PIECES = 8
 MESH = pl.DeviceIdType.MESH
 F32 = jnp.float32
 BF16 = jnp.bfloat16
@@ -236,12 +237,13 @@
             def _():
                 near_copy(chunk, 0).start()
 
-        for model in (STUDENT, TEACHER):
+        def arrive(model):
             near_copy(2 * g + model, 0).wait_recv()
             pltpu.make_async_copy(
                 (tq, sq)[model].at[0, :, pl.ds(0, WIDE)], qbuf.at[model, g], q_sem.at[model, g]
             ).wait()
 
+        arrive(STUDENT)
         slot = lax.rem(g, 2)
         triangle = wide_iota(0) <= lax.rem(wide_iota(1), rows)
         steps = [(model, hp) for model in (STUDENT, TEACHER) for hp in range(PAIRS)]
@@ -257,13 +259,14 @@
                 student = outs[STUDENT, g, :, cols].astype(F32)
                 ex_tx[g, :, cols] = (student - (1.0 + pipe_f) * mixed.astype(F32)).astype(BF16)
 
-        values_t = [win[2 * g + model, 1].T for model in (TEACHER, STUDENT)]
         later = raw_scores(*steps[0])
         pending = None
         for index, (model, hp) in enumerate(steps):
             cols = pl.ds(hp * PAIR, PAIR)
             raw = later
             if index + 1 < len(steps):
+                if steps[index + 1][0] != model:
+                    arrive(steps[index + 1][0])
                 later = raw_scores(*steps[index + 1])
             fill = bias[pl.ds(0, rows), :]
             middle = raw[rows : 2 * rows] + jnp.concatenate([fill, fill], axis=1)
@@ -286,7 +289,9 @@
                 rinv[g, :, cols] = inverse
             if pending is not None:
                 finish(*pending)
-            pending = (model, hp, dot(values_t[model], half), inverse)
+            if hp == 0:
+                values_t = win[2 * g + model, 1].T
+            pending = (model, hp, dot(values_t, half), inverse)
         finish(*pending)
         ex_copy(g).start()
 
@@ -404,6 +409,22 @@
         @pl.when(has_prev)
         def _():
             g2_copy(g).wait_send()
+
+
+def hand_over(qg_in, kg_in, vg_in, qg_out, kg_out, vg_out, sems):
+    part = qg_in.shape[1] // PIECES
+    copies = [
+        pltpu.make_async_copy(
+            qg_in.at[:, pl.ds(k * part, part), :], qg_out.at[:, pl.ds(k * part, part), :], sems.at[k]
+        )
+        for k in range(PIECES)
+    ]
+    copies.append(pltpu.make_async_copy(kg_in, kg_out, sems.at[PIECES]))
+    copies.append(pltpu.make_async_copy(vg_in, vg_out, sems.at[PIECES + 1]))
+    for copy in copies:
+        copy.start()
+    for copy in copies:
+        copy.wait()
 
 
 def per_device(count, pipes, t_query, t_key, t_value, s_query, s_key, s_value, segment_ids):
@@ -471,6 +492,15 @@
             transcendentals=2 * HEADS * rows * span,
         ),
     )(t_query, t_key, t_value, s_query, s_key, s_value, segment_ids.reshape(count, rows))
+    grads = (query_grad, key_grad, value_grad)
+    query_grad, key_grad, value_grad = pl.pallas_call(
+        hand_over,
+        out_shape=tuple(jax.ShapeDtypeStruct(grad.shape, F32) for grad in grads),
+        in_specs=[pl.BlockSpec(memory_space=pl.ANY)] * 3,
+        out_specs=(anywhere,) * 3,
+        scratch_shapes=[dma((PIECES + 2,))],
+        compiler_params=pltpu.CompilerParams(vmem_limit_bytes=63 * 1024 * 1024),
+    )(*grads)
     return loss.reshape(()), query_grad, key_grad, value_grad
 
 

time: 48.5 us -> 123 us (2.54)
  Pallas kernels: 41.3 us -> 121 us
  local copies, waits for them, and re-layouts: 4.58 us -> 0 us
    pallas_call x0 -> x1, Pallas kernels: none -> 80.6 us  [per_device(): pl.pallas_call(hand_over, out_shape=tuple((jax.ShapeDtypeStruct(grad.shap...]
    unnamed x7 -> x0, local copies, waits for them, and re-layouts: 4.58 us -> none
    pallas_call x1, Pallas kernels: 41.3 us -> 39.9 us  [per_device(): pl.pallas_call(functools.partial(kernel, count, rows, denominator), out_s...]
where the time goes in v3:
time: 123 us
  Pallas kernels  121 us (98%)
  between operations  2.33 us (2%)
    pallas_call x1, Pallas kernels, per_device(): pl.pallas_call(hand_over, out_shape=tuple((jax.ShapeDtypeStruct(grad.shap...  80.6 us
    pallas_call x1, Pallas kernels, per_device(): pl.pallas_call(functools.partial(kernel, count, rows, denominator), out_s...  39.9 us

profile of v3, /device:TPU:0, one launch (start us, length us, event | category | flops | bytes accessed | tf_op | source)
XLA Modules:
  0.0 122.8 jit_solution(9715343952548371515)
XLA Ops:
  0.6 39.9 %shard_map.102 = (f32[1,1]{1,0:T(1,128)}, f32[1,128,4096]{2,1,0:T(8,128)}, f32[1,128,512]{2,1,0:T(8,128)}, f32[1,128,512]{2,1,0:T(8,128)}) custom-call(bf16[1,128,4096]{2,1,0:T(8,128)(2,1)} %tq.1, bf16[1,128,512]{2,1,0:T(8,128)(2,1)} %tk.1, bf16[1,128,512]{2,1,0:T(8,128)(2,1)} %tv.1, bf16[1,128,4096]{2,1,0:T(8,128)(2,1)} %sq.1, bf16[1,128,512]{2,1,0:T(8,128)(2,1)} %sk.1, ...), custom_call_target="tpu_custom_call" | custom-call | flops 3221225472 | bytes 6291456 | tf_op jit(solution)/shard_map/pallas_call | solution.py:439
  40.6 80.6 %shard_map.103 = (f32[1,128,4096]{2,1,0:T(8,128)}, f32[1,128,512]{2,1,0:T(8,128)}, f32[1,128,512]{2,1,0:T(8,128)}) custom-call(f32[1,128,4096]{2,1,0:T(8,128)} %get-tuple-element.12.qg_in, f32[1,128,512]{2,1,0:T(8,128)} %get-tuple-element.13.kg_in, f32[1,128,512]{2,1,0:T(8,128)} %get-tuple-element.14.vg_in), custom_call_target="tpu_custom_call" | custom-call | tf_op jit(solution)/shard_map/pallas_call | solution.py:496

commit v4 on v3

--- a/solution.py
+++ b/solution.py
@@ -172,15 +172,17 @@
             device_id=(1 - pipe, me), device_id_type=MESH,
         )
 
-    def gx_copy(g):
+    def gx_copy(g, which):
         return pltpu.make_async_remote_copy(
-            src_ref=txx.at[g], dst_ref=rxx.at[g], send_sem=gx_send.at[g], recv_sem=gx_recv.at[g],
+            src_ref=txx.at[g, which], dst_ref=rxx.at[g, which],
+            send_sem=gx_send.at[g, which], recv_sem=gx_recv.at[g, which],
             device_id=(pipe, partner), device_id_type=MESH,
         )
 
-    def g2_copy(g):
+    def g2_copy(g, which):
         return pltpu.make_async_remote_copy(
-            src_ref=tx2.at[g], dst_ref=rx2.at[g], send_sem=g2_send.at[g], recv_sem=g2_recv.at[g],
+            src_ref=tx2.at[g, which], dst_ref=rx2.at[g, which],
+            send_sem=g2_send.at[g, which], recv_sem=g2_recv.at[g, which],
             device_id=(pipe, me - 2), device_id_type=MESH,
         )
 
@@ -295,6 +297,15 @@
         finish(*pending)
         ex_copy(g).start()
 
+    def pass_on(g):
+        for which in (1, 0):
+            gx_copy(g, which).wait_recv()
+            tx2[g, which] = (far_grad[g, which] + odd_f * rxx[g, which].astype(F32)).astype(BF16)
+
+            @pl.when(has_prev)
+            def _():
+                g2_copy(g, which).start()
+
     def backward(g):
         slot = lax.rem(g, 2)
         chunk = 2 * g + STUDENT
@@ -323,24 +334,29 @@
         def dprob_of(hp):
             return dot(win[chunk, 1], dnorm[:, pl.ds(hp * PAIR, PAIR)])
 
+        def split(which, grads):
+            txx[g, which] = grads[rows : 2 * rows].astype(BF16)
+            gx_copy(g, which).start()
+            far_grad[g, which] = grads[:rows]
+            own_grad[g, which] = grads[2 * rows :]
+
         later = dprob_of(0)
+        split(1, dot_nt(weights[slot], dnorm[...]))
+
+        @pl.when(g >= 1)
+        def _():
+            pass_on(g - 1)
+
         for hp in range(PAIRS):
             cols = pl.ds(hp * PAIR, PAIR)
             dprob = later
             if hp + 1 < PAIRS:
                 later = dprob_of(hp + 1)
-            else:
-                value_win = dot_nt(weights[slot], dnorm[...])
             dscore[:, cols] = (weights[slot, :, cols].astype(F32) * (dprob - delta[:, cols])).astype(BF16)
         queries = jnp.concatenate(
             [qbuf[STUDENT, g, :, pl.ds(h * HEAD_DIM, HEAD_DIM)] for h in range(GROUP)], axis=0
         )
-        key_win = dot(dscore[...], queries) * scale
-        for which, grads in enumerate((key_win, value_win)):
-            far_grad[g, which] = grads[:rows]
-            txx[g, which] = grads[rows : 2 * rows].astype(BF16)
-            own_grad[g, which] = grads[2 * rows :]
-        gx_copy(g).start()
+        split(0, dot(dscore[...], queries) * scale)
         keys_t = win[chunk, 0].T
         for hp in range(PAIRS):
             query_t = dot(keys_t, dscore[:, pl.ds(hp * PAIR, PAIR)]) * scale
@@ -348,14 +364,6 @@
             qgrad[g, :, pl.ds(hp * PAIR + HEAD_DIM, HEAD_DIM)] = query_t[:, HEAD_DIM:].T
         qg_copy(g).start()
 
-    def pass_on(g):
-        gx_copy(g).wait_recv()
-        tx2[g] = (far_grad[g] + odd_f * rxx[g].astype(F32)).astype(BF16)
-
-        @pl.when(has_prev)
-        def _():
-            g2_copy(g).start()
-
     def step(g, carry):
         @pl.when(g < KV_HEADS)
         def _():
@@ -364,10 +372,6 @@
         @pl.when(g >= 1)
         def _():
             backward(g - 1)
-
-        @pl.when(g >= 2)
-        def _():
-            pass_on(g - 2)
 
         return carry
 
@@ -386,7 +390,8 @@
 
         @pl.when(has_next)
         def _():
-            g2_copy(g).wait_recv()
+            g2_copy(g, 0).wait_recv()
+            g2_copy(g, 1).wait_recv()
 
         cols = pl.ds(g * HEAD_DIM, HEAD_DIM)
         for which, out in enumerate((kg_out, vg_out)):
@@ -403,28 +408,30 @@
 
     for g in range(KV_HEADS):
         ex_copy(g).wait_send()
-        gx_copy(g).wait_send()
+        gx_copy(g, 0).wait_send()
+        gx_copy(g, 1).wait_send()
         qg_copy(g).wait()
 
         @pl.when(has_prev)
         def _():
-            g2_copy(g).wait_send()
-
-
-def hand_over(qg_in, kg_in, vg_in, qg_out, kg_out, vg_out, sems):
+            g2_copy(g, 0).wait_send()
+            g2_copy(g, 1).wait_send()
+
+
+def hand_over(qg_in, kg_in, vg_in, qg_out, kg_out, vg_out, qg_held, kg_held, vg_held, sems_in, sems_out):
     part = qg_in.shape[1] // PIECES
-    copies = [
-        pltpu.make_async_copy(
-            qg_in.at[:, pl.ds(k * part, part), :], qg_out.at[:, pl.ds(k * part, part), :], sems.at[k]
-        )
-        for k in range(PIECES)
-    ]
-    copies.append(pltpu.make_async_copy(kg_in, kg_out, sems.at[PIECES]))
-    copies.append(pltpu.make_async_copy(vg_in, vg_out, sems.at[PIECES + 1]))
-    for copy in copies:
-        copy.start()
-    for copy in copies:
-        copy.wait()
+    rows_of = [pl.ds(k * part, part) for k in range(PIECES)]
+    ways = [(qg_in.at[:, r, :], qg_held.at[:, r, :], qg_out.at[:, r, :]) for r in rows_of]
+    ways += [(kg_in, kg_held, kg_out), (vg_in, vg_held, vg_out)]
+    loads = [pltpu.make_async_copy(src, held, sems_in.at[k]) for k, (src, held, _) in enumerate(ways)]
+    stores = [pltpu.make_async_copy(held, dst, sems_out.at[k]) for k, (_, held, dst) in enumerate(ways)]
+    for load in loads:
+        load.start()
+    for load, store in zip(loads, stores):
+        load.wait()
+        store.start()
+    for store in stores:
+        store.wait()
 
 
 def per_device(count, pipes, t_query, t_key, t_value, s_query, s_key, s_value, segment_ids):
@@ -476,10 +483,10 @@
             dma((2 * KV_HEADS,)),
             dma((KV_HEADS,)),
             dma((KV_HEADS,)),
-            dma((KV_HEADS,)),
-            dma((KV_HEADS,)),
-            dma((KV_HEADS,)),
-            dma((KV_HEADS,)),
+            dma((KV_HEADS, 2)),
+            dma((KV_HEADS, 2)),
+            dma((KV_HEADS, 2)),
+            dma((KV_HEADS, 2)),
             dma((rounds, 8)),
             dma((rounds, 8)),
         ],
@@ -498,7 +505,7 @@
         out_shape=tuple(jax.ShapeDtypeStruct(grad.shape, F32) for grad in grads),
         in_specs=[pl.BlockSpec(memory_space=pl.ANY)] * 3,
         out_specs=(anywhere,) * 3,
-        scratch_shapes=[dma((PIECES + 2,))],
+        scratch_shapes=[pltpu.VMEM(grad.shape, F32) for grad in grads] + [dma((PIECES + 2,))] * 2,
         compiler_params=pltpu.CompilerParams(vmem_limit_bytes=63 * 1024 * 1024),
     )(*grads)
     return loss.reshape(()), query_grad, key_grad, value_grad

time: 123 us -> 50.4 us (0.41)
  Pallas kernels: 121 us -> 47.9 us
    pallas_call x1, Pallas kernels: 80.6 us -> 2.6 us  [per_device(): pl.pallas_call(hand_over, out_shape=tuple((jax.ShapeDtypeStruct(grad.shap...]
    pallas_call x1, Pallas kernels: 39.9 us -> 45.3 us  [per_device(): pl.pallas_call(functools.partial(kernel, count, rows, denominator), out_s...]
where the time goes in v4:
time: 50.4 us; the launch traced here: 50.2 us
  Pallas kernels  47.9 us (95%)
  between operations  2.33 us (5%)
    pallas_call x1, Pallas kernels, per_device(): pl.pallas_call(functools.partial(kernel, count, rows, denominator), out_s...  45.3 us
    pallas_call x1, Pallas kernels, per_device(): pl.pallas_call(hand_over, out_shape=tuple((jax.ShapeDtypeStruct(grad.shap...  2.6 us

profile of v4, /device:TPU:0, one launch (start us, length us, event | category | flops | bytes accessed | tf_op | source)
XLA Modules:
  0.0 50.2 jit_solution(7628359291309987462)
XLA Ops:
  0.6 45.3 %shard_map.102 = (f32[1,1]{1,0:T(1,128)}, f32[1,128,4096]{2,1,0:T(8,128)}, f32[1,128,512]{2,1,0:T(8,128)}, f32[1,128,512]{2,1,0:T(8,128)}) custom-call(bf16[1,128,4096]{2,1,0:T(8,128)(2,1)} %tq.1, bf16[1,128,512]{2,1,0:T(8,128)(2,1)} %tk.1, bf16[1,128,512]{2,1,0:T(8,128)(2,1)} %tv.1, bf16[1,128,4096]{2,1,0:T(8,128)(2,1)} %sq.1, bf16[1,128,512]{2,1,0:T(8,128)(2,1)} %sk.1, ...), custom_call_target="tpu_custom_call" | custom-call | flops 3221225472 | bytes 6291456 | tf_op jit(solution)/shard_map/pallas_call | solution.py:446
  45.9 2.6 %shard_map.103 = (f32[1,128,4096]{2,1,0:T(8,128)}, f32[1,128,512]{2,1,0:T(8,128)}, f32[1,128,512]{2,1,0:T(8,128)}) custom-call(f32[1,128,4096]{2,1,0:T(8,128)} %get-tuple-element.12.qg_in, f32[1,128,512]{2,1,0:T(8,128)} %get-tuple-element.13.kg_in, f32[1,128,512]{2,1,0:T(8,128)} %get-tuple-element.14.vg_in), custom_call_target="tpu_custom_call" | custom-call | tf_op jit(solution)/shard_map/pallas_call | solution.py:503

commit v5 on v3

--- a/solution.py
+++ b/solution.py
@@ -411,20 +411,20 @@
             g2_copy(g).wait_send()
 
 
-def hand_over(qg_in, kg_in, vg_in, qg_out, kg_out, vg_out, sems):
+def hand_over(qg_in, kg_in, vg_in, qg_out, kg_out, vg_out, qg_held, kg_held, vg_held, sems_in, sems_out):
     part = qg_in.shape[1] // PIECES
-    copies = [
-        pltpu.make_async_copy(
-            qg_in.at[:, pl.ds(k * part, part), :], qg_out.at[:, pl.ds(k * part, part), :], sems.at[k]
-        )
-        for k in range(PIECES)
-    ]
-    copies.append(pltpu.make_async_copy(kg_in, kg_out, sems.at[PIECES]))
-    copies.append(pltpu.make_async_copy(vg_in, vg_out, sems.at[PIECES + 1]))
-    for copy in copies:
-        copy.start()
-    for copy in copies:
-        copy.wait()
+    rows_of = [pl.ds(k * part, part) for k in range(PIECES)]
+    ways = [(qg_in.at[:, r, :], qg_held.at[:, r, :], qg_out.at[:, r, :]) for r in rows_of]
+    ways += [(kg_in, kg_held, kg_out), (vg_in, vg_held, vg_out)]
+    loads = [pltpu.make_async_copy(src, held, sems_in.at[k]) for k, (src, held, _) in enumerate(ways)]
+    stores = [pltpu.make_async_copy(held, dst, sems_out.at[k]) for k, (_, held, dst) in enumerate(ways)]
+    for load in loads:
+        load.start()
+    for load, store in zip(loads, stores):
+        load.wait()
+        store.start()
+    for store in stores:
+        store.wait()
 
 
 def per_device(count, pipes, t_query, t_key, t_value, s_query, s_key, s_value, segment_ids):
@@ -498,7 +498,7 @@
         out_shape=tuple(jax.ShapeDtypeStruct(grad.shape, F32) for grad in grads),
         in_specs=[pl.BlockSpec(memory_space=pl.ANY)] * 3,
         out_specs=(anywhere,) * 3,
-        scratch_shapes=[dma((PIECES + 2,))],
+        scratch_shapes=[pltpu.VMEM(grad.shape, F32) for grad in grads] + [dma((PIECES + 2,))] * 2,
         compiler_params=pltpu.CompilerParams(vmem_limit_bytes=63 * 1024 * 1024),
     )(*grads)
     return loss.reshape(()), query_grad, key_grad, value_grad

time: 123 us -> 45.1 us (0.37)
  Pallas kernels: 121 us -> 42.5 us
    pallas_call x1, Pallas kernels: 80.6 us -> 2.6 us  [per_device(): pl.pallas_call(hand_over, out_shape=tuple((jax.ShapeDtypeStruct(grad.shap...]
where the time goes in v5:
time: 45.1 us; the launch traced here: 44.8 us
  Pallas kernels  42.5 us (94%)
  between operations  2.33 us (5%)
    pallas_call x1, Pallas kernels, per_device(): pl.pallas_call(functools.partial(kernel, count, rows, denominator), out_s...  39.9 us
    pallas_call x1, Pallas kernels, per_device(): pl.pallas_call(hand_over, out_shape=tuple((jax.ShapeDtypeStruct(grad.shap...  2.6 us

profile of v5, /device:TPU:0, one launch (start us, length us, event | category | flops | bytes accessed | tf_op | source)
XLA Modules:
  0.0 44.8 jit_solution(7278851000476417985)
XLA Ops:
  0.6 39.9 %shard_map.102 = (f32[1,1]{1,0:T(1,128)}, f32[1,128,4096]{2,1,0:T(8,128)}, f32[1,128,512]{2,1,0:T(8,128)}, f32[1,128,512]{2,1,0:T(8,128)}) custom-call(bf16[1,128,4096]{2,1,0:T(8,128)(2,1)} %tq.1, bf16[1,128,512]{2,1,0:T(8,128)(2,1)} %tk.1, bf16[1,128,512]{2,1,0:T(8,128)(2,1)} %tv.1, bf16[1,128,4096]{2,1,0:T(8,128)(2,1)} %sq.1, bf16[1,128,512]{2,1,0:T(8,128)(2,1)} %sk.1, ...), custom_call_target="tpu_custom_call" | custom-call | flops 3221225472 | bytes 6291456 | tf_op jit(solution)/shard_map/pallas_call | solution.py:439
  40.6 2.6 %shard_map.103 = (f32[1,128,4096]{2,1,0:T(8,128)}, f32[1,128,512]{2,1,0:T(8,128)}, f32[1,128,512]{2,1,0:T(8,128)}) custom-call(f32[1,128,4096]{2,1,0:T(8,128)} %get-tuple-element.12.qg_in, f32[1,128,512]{2,1,0:T(8,128)} %get-tuple-element.13.kg_in, f32[1,128,512]{2,1,0:T(8,128)} %get-tuple-element.14.vg_in), custom_call_target="tpu_custom_call" | custom-call | tf_op jit(solution)/shard_map/pallas_call | solution.py:496

commit v6 on v4

--- a/solution.py
+++ b/solution.py
@@ -343,10 +343,6 @@
         later = dprob_of(0)
         split(1, dot_nt(weights[slot], dnorm[...]))
 
-        @pl.when(g >= 1)
-        def _():
-            pass_on(g - 1)
-
         for hp in range(PAIRS):
             cols = pl.ds(hp * PAIR, PAIR)
             dprob = later
@@ -372,6 +368,10 @@
         @pl.when(g >= 1)
         def _():
             backward(g - 1)
+
+        @pl.when(g >= 2)
+        def _():
+            pass_on(g - 2)
 
         return carry
 

time: 50.4 us -> 46.2 us (0.917)
  Pallas kernels: 47.9 us -> 43.6 us
    pallas_call x1, Pallas kernels: 45.3 us -> 41 us  [per_device(): pl.pallas_call(functools.partial(kernel, count, rows, denominator), out_s...]
where the time goes in v6:
time: 46.2 us; the launch traced here: 46 us
  Pallas kernels  43.6 us (94%)
  between operations  2.33 us (5%)
    pallas_call x1, Pallas kernels, per_device(): pl.pallas_call(functools.partial(kernel, count, rows, denominator), out_s...  41 us
    pallas_call x1, Pallas kernels, per_device(): pl.pallas_call(hand_over, out_shape=tuple((jax.ShapeDtypeStruct(grad.shap...  2.6 us

profile of v6, /device:TPU:0, one launch (start us, length us, event | category | flops | bytes accessed | tf_op | source)
XLA Modules:
  0.0 46.0 jit_solution(4214960331411993048)
XLA Ops:
  0.6 41.0 %shard_map.102 = (f32[1,1]{1,0:T(1,128)}, f32[1,128,4096]{2,1,0:T(8,128)}, f32[1,128,512]{2,1,0:T(8,128)}, f32[1,128,512]{2,1,0:T(8,128)}) custom-call(bf16[1,128,4096]{2,1,0:T(8,128)(2,1)} %tq.1, bf16[1,128,512]{2,1,0:T(8,128)(2,1)} %tk.1, bf16[1,128,512]{2,1,0:T(8,128)(2,1)} %tv.1, bf16[1,128,4096]{2,1,0:T(8,128)(2,1)} %sq.1, bf16[1,128,512]{2,1,0:T(8,128)(2,1)} %sk.1, ...), custom_call_target="tpu_custom_call" | custom-call | flops 3221225472 | bytes 6291456 | tf_op jit(solution)/shard_map/pallas_call | solution.py:446
  41.7 2.6 %shard_map.103 = (f32[1,128,4096]{2,1,0:T(8,128)}, f32[1,128,512]{2,1,0:T(8,128)}, f32[1,128,512]{2,1,0:T(8,128)}) custom-call(f32[1,128,4096]{2,1,0:T(8,128)} %get-tuple-element.12.qg_in, f32[1,128,512]{2,1,0:T(8,128)} %get-tuple-element.13.kg_in, f32[1,128,512]{2,1,0:T(8,128)} %get-tuple-element.14.vg_in), custom_call_target="tpu_custom_call" | custom-call | tf_op jit(solution)/shard_map/pallas_call | solution.py:503
